TPU v7x, 256 devices: a whole 4x4x8 slice. The times are simulated.
256 devices in a mesh: section: 16 (over x_hi, y, core), dp: 16 (over x_lo, z).
Axes of the slice: x: 4 (x_hi: 2, x_lo: 2; x = x_hi * 2 + x_lo), y: 4, z: 8, core: 2. Of those that a mesh axis runs over, the one named last changes fastest.
Arguments:
- micro_inputs: bfloat16 [2, 4, 256, 8192], P(None, None, 'dp'), may hold values from -6 to 6
- cotangent: bfloat16 [2, 4, 256, 8192], P(None, None, 'dp'), may hold values from -6 to 6
- norm_gain: bfloat16 [16, 8192], P('section'), may hold values from 0.5 to 1.5
- enter_weight: float32 [16, 8192, 128], P('section', 'dp'), may hold values from -0.0625 to 0.0625
- enter_moment: float32 [16, 8192, 128], P('section', 'dp'), may hold values from -150 to 150
- enter_second: float32 [16, 8192, 128], P('section', 'dp'), may hold values from 1000 to 100000
- leave_weight: float32 [16, 128, 8192], P('section', None, 'dp'), may hold values from -0.5 to 0.5
- leave_moment: float32 [16, 128, 8192], P('section', None, 'dp'), may hold values from -12 to 12
- leave_second: float32 [16, 128, 8192], P('section', None, 'dp'), may hold values from 10 to 1000
Outputs:
- new_enter_weight: float32 [16, 8192, 128], P('section', 'dp')
- new_enter_moment: float32 [16, 8192, 128], P('section', 'dp')
- new_enter_second: float32 [16, 8192, 128], P('section', 'dp')
- new_leave_weight: float32 [16, 128, 8192], P('section', None, 'dp')
- new_leave_moment: float32 [16, 128, 8192], P('section', None, 'dp')
- new_leave_second: float32 [16, 128, 8192], P('section', None, 'dp')
All inputs are finite; a program needn't handle non-finite values.
Results may differ from a plain program's by a relative error of at most 0.04.
Values may be sent and summed in bfloat16 or wider, within the bound.
No kernel may reach another device: no remote copies, remote signals or barrier semaphores. Data moves between devices by JAX's collectives and lax.ppermute only.
A program may use at most 64 MiB of HBM per device.

v0:
```python
import jax
import jax.numpy as jnp
from jax import lax
from jax.sharding import PartitionSpec as P

eps_norm = 1e-05
rate = 0.001
beta_one = 0.9
beta_two = 0.95
adam_eps = 1e-08
step_count = 10


def partner(value, axis, distance):
    mask = 2**distance
    pairs = [(source, source ^ mask) for source in range(lax.axis_size(axis))]
    return lax.ppermute(value, axis, pairs)


def from_behind(value, axis, by):
    devices = lax.axis_size(axis)
    pairs = [(i, i + by) for i in range(devices) if 0 <= i + by < devices]
    return lax.ppermute(value, axis, pairs)


def layer_inner(layer_rows, enter_mat, gain_row):
    wide_rows = layer_rows.astype(jnp.float32)
    inverse = lax.rsqrt(jnp.mean(wide_rows * wide_rows, axis=-1, keepdims=True) + eps_norm)
    normed = (wide_rows * inverse * gain_row.astype(jnp.float32)).astype(jnp.bfloat16)
    pre_act = jnp.dot(normed, enter_mat, preferred_element_type=jnp.float32)
    return (wide_rows, inverse, normed, pre_act)


def layer_forward(layer_rows, enter_mat, leave_mat, gain_row):
    wide_rows, inverse, normed, pre_act = layer_inner(layer_rows, enter_mat, gain_row)
    hidden = jax.nn.silu(pre_act).astype(jnp.bfloat16)
    branch = jnp.dot(hidden, leave_mat, preferred_element_type=jnp.float32)
    return (wide_rows + branch).astype(jnp.bfloat16)


def layer_backward(layer_rows, incoming, enter_mat, leave_mat, gain_row):
    wide_rows, inverse, normed, pre_act = layer_inner(layer_rows, enter_mat, gain_row)
    hidden_grad = lax.dot_general(
        incoming, leave_mat, (((1,), (1,)), ((), ())), preferred_element_type=jnp.float32
    )
    sig_act = jax.nn.sigmoid(pre_act)
    inner_grad = (hidden_grad * sig_act * (1.0 + pre_act * (1.0 - sig_act))).astype(jnp.bfloat16)
    normed_grad = lax.dot_general(
        inner_grad, enter_mat, (((1,), (1,)), ((), ())), preferred_element_type=jnp.float32
    )
    scaled = normed_grad * gain_row.astype(jnp.float32)
    mean_term = jnp.mean(scaled * wide_rows, axis=-1, keepdims=True)
    outgoing = (
        incoming.astype(jnp.float32)
        + inverse * scaled
        - wide_rows * (inverse * inverse * inverse) * mean_term
    )
    return (outgoing.astype(jnp.bfloat16), inner_grad)


def adam_update(weight, moment, second, grad):
    moment_new = beta_one * moment + (1.0 - beta_one) * grad
    second_new = beta_two * second + (1.0 - beta_two) * grad * grad
    corr_one = 1.0 - beta_one**step_count
    corr_two = 1.0 - beta_two**step_count
    weight_new = weight - rate * (moment_new / corr_one) / (
        jnp.sqrt(second_new / corr_two) + adam_eps
    )
    return (weight_new, moment_new, second_new)


def record(saved_rows, update_rows, slot_index, batches):
    is_valid = (slot_index >= 0) & (slot_index < batches)
    slot_clip = jnp.clip(slot_index, 0, batches - 1)
    previous = lax.dynamic_index_in_dim(saved_rows, slot_clip, 0, keepdims=False)
    return lax.dynamic_update_index_in_dim(
        saved_rows, jnp.where(is_valid, update_rows, previous), slot_clip, 0
    )


def is_active(slot_index, batches):
    return (slot_index >= 0) & (slot_index < batches)


def forward_when(active, rows_in, enter_mat, leave_mat, gain_row):

    def forward_run_layer(operands):
        return layer_forward(operands[0], enter_mat, leave_mat, gain_row)

    def forward_skip_layer(operands):
        return jnp.zeros_like(operands[0])

    return lax.cond(active, forward_run_layer, forward_skip_layer, (rows_in,))


def backward_when(active, rows_in, incoming, enter_mat, leave_mat, gain_row, rank_units):

    def backward_run_layer(operands):
        return layer_backward(operands[0], operands[1], enter_mat, leave_mat, gain_row)

    def backward_skip_layer(operands):
        return (
            jnp.zeros_like(operands[1]),
            jnp.zeros((operands[1].shape[0], rank_units), jnp.bfloat16),
        )

    return lax.cond(active, backward_run_layer, backward_skip_layer, (rows_in, incoming))


def reverse_weights(enter_part, leave_part, gain_part):
    for bit_index in range(lax.axis_size("section").bit_length() - 1):
        enter_part, leave_part, gain_part = partner(
            (enter_part, leave_part, gain_part), "section", bit_index
        )
    return (enter_part, leave_part, gain_part)


def reverse_grads(grad_part):
    for bit_index in range(lax.axis_size("section").bit_length() - 1):
        grad_part = partner(grad_part.astype(jnp.bfloat16), "section", bit_index).astype(
            grad_part.dtype
        )
    return grad_part


def per_device(
    micro_inputs,
    cotangent,
    norm_gain,
    enter_weight,
    enter_moment,
    enter_second,
    leave_weight,
    leave_moment,
    leave_second,
):
    section_index = lax.axis_index("section")
    section_count = lax.axis_size("section")
    mirror = section_count - 1 - section_index
    batches = micro_inputs.shape[1]
    rows_micro = micro_inputs.shape[2]
    model_width = micro_inputs.shape[3]
    rank_units = enter_weight.shape[2]
    own_enter = enter_weight.astype(jnp.bfloat16)
    own_leave = leave_weight.astype(jnp.bfloat16)
    far_enter, far_leave, far_gain = reverse_weights(own_enter, own_leave, norm_gain)
    enter_down, leave_down, enter_up, leave_up = (
        lax.all_gather(own_enter[0], "dp", axis=0, tiled=True),
        lax.all_gather(own_leave[0], "dp", axis=1, tiled=True),
        lax.all_gather(far_enter[0], "dp", axis=0, tiled=True),
        lax.all_gather(far_leave[0], "dp", axis=1, tiled=True),
    )
    gain_down = norm_gain[0]
    gain_up = far_gain[0]
    empty_rows = jnp.zeros((rows_micro, model_width), jnp.bfloat16)
    empty_saved = jnp.zeros((batches, rows_micro, model_width), jnp.bfloat16)
    empty_inner = jnp.zeros((batches, rows_micro, rank_units), jnp.bfloat16)
    tick_total = section_count + batches - 1

    def forward_tick(tick_index, loop_state):
        down_recv, up_recv, saved_down, saved_up = loop_state
        pick_index = jnp.clip(tick_index, 0, batches - 1)
        fresh_down = lax.dynamic_index_in_dim(micro_inputs[0], pick_index, 0, keepdims=False)
        fresh_up = lax.dynamic_index_in_dim(micro_inputs[1], pick_index, 0, keepdims=False)
        down_in = jnp.where(section_index == 0, fresh_down, down_recv)
        up_in = jnp.where(mirror == 0, fresh_up, up_recv)
        down_slot = tick_index - section_index
        up_slot = tick_index - mirror
        saved_down = record(saved_down, down_in, down_slot, batches)
        saved_up = record(saved_up, up_in, up_slot, batches)
        down_out = forward_when(
            is_active(down_slot, batches), down_in, enter_down, leave_down, gain_down
        )
        up_out = forward_when(is_active(up_slot, batches), up_in, enter_up, leave_up, gain_up)
        down_next = from_behind(down_out, "section", 1)
        up_next = from_behind(up_out, "section", -1)
        return (down_next, up_next, saved_down, saved_up)

    forward_state = lax.fori_loop(
        0, tick_total, forward_tick, (empty_rows, empty_rows, empty_saved, empty_saved)
    )
    saved_down = forward_state[2]
    saved_up = forward_state[3]

    def backward_tick(tick_index, loop_state):
        down_recv, up_recv, grads_down, grads_up, inner_down, inner_up = loop_state
        pick_index = jnp.clip(tick_index, 0, batches - 1)
        fresh_down = lax.dynamic_index_in_dim(cotangent[0], pick_index, 0, keepdims=False)
        fresh_up = lax.dynamic_index_in_dim(cotangent[1], pick_index, 0, keepdims=False)
        down_in = jnp.where(mirror == 0, fresh_down, down_recv)
        up_in = jnp.where(section_index == 0, fresh_up, up_recv)
        down_slot = tick_index - mirror
        up_slot = tick_index - section_index
        rows_down = lax.dynamic_index_in_dim(
            saved_down, jnp.clip(down_slot, 0, batches - 1), 0, keepdims=False
        )
        rows_up = lax.dynamic_index_in_dim(
            saved_up, jnp.clip(up_slot, 0, batches - 1), 0, keepdims=False
        )
        back_down, pre_grad_down = backward_when(
            is_active(down_slot, batches),
            rows_down,
            down_in,
            enter_down,
            leave_down,
            gain_down,
            rank_units,
        )
        back_up, pre_grad_up = backward_when(
            is_active(up_slot, batches), rows_up, up_in, enter_up, leave_up, gain_up, rank_units
        )
        grads_down = record(grads_down, down_in, down_slot, batches)
        grads_up = record(grads_up, up_in, up_slot, batches)
        inner_down = record(inner_down, pre_grad_down, down_slot, batches)
        inner_up = record(inner_up, pre_grad_up, up_slot, batches)
        down_next = from_behind(back_down, "section", -1)
        up_next = from_behind(back_up, "section", 1)
        return (down_next, up_next, grads_down, grads_up, inner_down, inner_up)

    backward_state = lax.fori_loop(
        0,
        tick_total,
        backward_tick,
        (empty_rows, empty_rows, empty_saved, empty_saved, empty_inner, empty_inner),
    )
    grads_down, grads_up, inner_down, inner_up = backward_state[2:]

    def flatten_side(saved_rows, saved_grad, saved_inner, enter_mat, gain_row):
        flat_in = saved_rows.reshape(-1, model_width)
        wide_rows, inverse, normed, pre_act = layer_inner(flat_in, enter_mat, gain_row)
        hidden = jax.nn.silu(pre_act).astype(jnp.bfloat16)
        return (
            normed,
            hidden,
            saved_grad.reshape(-1, model_width),
            saved_inner.reshape(-1, rank_units),
        )

    side_down = flatten_side(saved_down, grads_down, inner_down, enter_down, gain_down)
    side_up = flatten_side(saved_up, grads_up, inner_up, enter_up, gain_up)
    contract_rows = (((0,), (0,)), ((), ()))
    pieces = []
    for normed, hidden, flat_grad, flat_inner in (side_down, side_up):
        pieces.append(
            lax.dot_general(normed, flat_inner, contract_rows, preferred_element_type=jnp.float32)
        )
        pieces.append(
            lax.dot_general(flat_grad, hidden, contract_rows, preferred_element_type=jnp.float32)
        )
    shares = lax.psum_scatter(
        jnp.concatenate(pieces, axis=1).astype(jnp.bfloat16), "dp", scatter_dimension=0, tiled=True
    ).astype(jnp.float32)
    down_part = shares[:, : 2 * rank_units]
    up_part = shares[:, 2 * rank_units :]
    total_grad = down_part + reverse_grads(up_part)
    enter_grad = total_grad[:, :rank_units]
    leave_grad = total_grad[:, rank_units:].T
    new_enter, new_enter_moment, new_enter_second = adam_update(
        enter_weight[0], enter_moment[0], enter_second[0], enter_grad
    )
    new_leave, new_leave_moment, new_leave_second = adam_update(
        leave_weight[0], leave_moment[0], leave_second[0], leave_grad
    )
    return (
        new_enter[None],
        new_enter_moment[None],
        new_enter_second[None],
        new_leave[None],
        new_leave_moment[None],
        new_leave_second[None],
    )


def solution(mesh):
    return jax.shard_map(
        per_device,
        mesh=mesh,
        in_specs=(
            P(None, None, "dp", None),
            P(None, None, "dp", None),
            P("section", None),
            P("section", "dp", None),
            P("section", "dp", None),
            P("section", "dp", None),
            P("section", None, "dp"),
            P("section", None, "dp"),
            P("section", None, "dp"),
        ),
        out_specs=(
            P("section", "dp", None),
            P("section", "dp", None),
            P("section", "dp", None),
            P("section", None, "dp"),
            P("section", None, "dp"),
            P("section", None, "dp"),
        ),
        check_vma=False,
    )
```

profile of v0, /device:TPU:8, one launch (start us, length us, event | category | flops | bytes accessed | tf_op | source)
XLA Modules:
  0.0 1458.6 jit_solution(16020573250641919620)
XLA Ops:
  71.1 13.6 all-gather.9.cloned.1.call-done
  84.8 71.6 %all-gather.11.cloned.1.call-done = bf16[1,128,8192]{2,1,0:T(8,128)(2,1)} async-done(((bf16[1,128,512]{2,1,0:T(8,128)(2,1)}), bf16[1,128,8192]{2,1,0:T(8,128)(2,1)}) %all-gather.11.cloned.1.call-update) | async-done | bytes 2097168 | tf_op jit(solution)/shard_map/all_gather | solution.py:149
  156.3 71.3 %all-gather.13.cloned.1.call-done = bf16[1,8192,128]{2,1,0:T(8,128)(2,1)} async-done(((bf16[1,512,128]{2,1,0:T(8,128)(2,1)}), bf16[1,8192,128]{2,1,0:T(8,128)(2,1)}) %all-gather.13.cloned.1.call-update) | async-done | bytes 2097168 | tf_op jit(solution)/shard_map/all_gather | solution.py:150
  227.6 70.9 %all-gather.15.cloned.1.call-done = bf16[1,128,8192]{2,1,0:T(8,128)(2,1)} async-done(((bf16[1,128,512]{2,1,0:T(8,128)(2,1)}), bf16[1,128,8192]{2,1,0:T(8,128)(2,1)}) %all-gather.15.cloned.1.call-update) | async-done | bytes 2097168 | tf_op jit(solution)/shard_map/all_gather | solution.py:151
  301.1 425.5 %while.44 = (s32[]{:T(128)}, bf16[16,8192]{1,0:T(8,128)(2,1)}, bf16[16,8192]{1,0:T(8,128)(2,1)}, bf16[4,16,8192]{2,1,0:T(8,128)(2,1)S(1)}, bf16[4,16,8192]{2,1,0...) while((s32[]{:T(128)}, bf16[16,8192]{1,0:T(8,128)(2,1)}, ...), condition=%wide.region_7.8_spmd, body=%wide.region_0.7_spmd.sunk | while | flops 137400352 | bytes 21136928 | solution.py:179
  531.8 7.3 collective-permute-start
  551.6 29.6 %collective-permute-start = (bf16[16,8192]{1,0:T(8,128)(2,1)}, bf16[16,8192]{1,0:T(8,128)(2,1)S(1)}, u32[]{:S(2)}, u32[]{:S(2)}) collective-permute-start(bf16[16,8192]{1,0:T(8,128)(2,1)} %get-tuple-element.1292), channel_id=1, source_target_pairs={{0,16},{16,32},{32,48},{48,64},{64,80},{80,96},{96,112},{112,128},... | collective-permute-start | bytes 786440 | tf_op jit(solution)/shard_map/while/body/eval_jaxpr/ppermute | solution.py:23
  597.0 10.2 collective-permute-start
  622.9 12.8 collective-permute-start
  651.5 10.1 collective-permute-start
  733.5 564.6 %while.45 = (s32[]{:T(128)}, bf16[16,8192]{1,0:T(8,128)(2,1)}, bf16[16,8192]{1,0:T(8,128)(2,1)}, bf16[4,16,8192]{2,1,0:T(8,128)(2,1)}, bf16[4,16,8192]{2,1,0:T(8...) while((s32[]{:T(128)}, bf16[16,8192]{1,0:T(8,128)(2,1)}, ...), condition=%wide.region_18.19_spmd, body=%wide.region_9.18_spmd.sunk | while | flops 206889056 | bytes 54850600 | solution.py:220
  751.0 7.1 collective-permute-done.2
  765.9 13.2 collective-permute-start.3
  796.0 8.5 conditional.11
  804.4 9.0 collective-permute-start.3
  830.3 8.5 conditional.11
  838.7 13.3 collective-permute-start.3
  868.9 8.5 conditional.11
  897.9 8.5 conditional.11
  928.1 10.8 collective-permute-start.3
  967.0 8.2 collective-permute-done.2
  983.1 6.7 collective-permute-start.3
  1007.9 7.5 collective-permute-start.3
  1057.6 20.6 %collective-permute-start.3 = (bf16[16,8192]{1,0:T(8,128)(2,1)}, bf16[16,8192]{1,0:T(8,128)(2,1)}, u32[]{:S(2)}, u32[]{:S(2)}) collective-permute-start(bf16[16,8192]{1,0:T(8,128)(2,1)} %get-tuple-element.1145), channel_id=1, source_target_pairs={{0,16},{16,32},{32,48},{48,64},{64,80},{80,96},{96,112},{112,128},... | collective-permute-start | bytes 786440 | tf_op jit(solution)/shard_map/while/body/eval_jaxpr/ppermute | solution.py:23
  1096.4 22.3 %collective-permute-start.3 = (bf16[16,8192]{1,0:T(8,128)(2,1)}, bf16[16,8192]{1,0:T(8,128)(2,1)}, u32[]{:S(2)}, u32[]{:S(2)}) collective-permute-start(bf16[16,8192]{1,0:T(8,128)(2,1)} %get-tuple-element.1145), channel_id=1, source_target_pairs={{0,16},{16,32},{32,48},{48,64},{64,80},{80,96},{96,112},{112,128},... | collective-permute-start | bytes 786440 | tf_op jit(solution)/shard_map/while/body/eval_jaxpr/ppermute | solution.py:23
  1137.8 9.8 collective-permute-start.3
  1169.7 14.4 collective-permute-start.3
  1263.7 7.6 collective-permute-start.2
  1313.1 6.6 pad_maximum_fusion
  1319.8 100.1 %reduce-scatter.2.cloned.1.call-done = bf16[512,512]{0,1:T(8,128)(2,1)} async-done(((bf16[8192,512]{0,1:T(8,128)(2,1)}), bf16[512,512]{0,1:T(8,128)(2,1)}) %reduce-scatter.2.cloned.1.call-update) | async-done | bytes 524304 | tf_op jit(solution)/shard_map/reduce_scatter | solution.py:250
  1423.3 7.8 collective-permute-done.17
  1433.2 6.9 collective-permute-done.18
  (850 shorter events, 983.9 us)
Async XLA Ops:
  7.2 77.6 %all-gather.9.cloned.1.call-start = ((), (), s32[]{:S(2)}) async-start(), calls=%async_computation.2 | async-start | bytes 2228224 | tf_op jit(solution)/shard_map/all_gather | solution.py:148
  8.9 147.5 %all-gather.11.cloned.1.call-start = ((), (), s32[]{:S(2)}) async-start(), calls=%async_computation.3 | async-start | bytes 2228224 | tf_op jit(solution)/shard_map/all_gather | solution.py:149
  10.6 217.1 %all-gather.13.cloned.1.call-start = ((), (), s32[]{:S(2)}) async-start(), calls=%async_computation.4 | async-start | bytes 2228224 | tf_op jit(solution)/shard_map/all_gather | solution.py:150
  33.3 265.2 %all-gather.15.cloned.1.call-start = ((), (), s32[]{:S(2)}) async-start(), calls=%async_computation.5 | async-start | bytes 2228224 | tf_op jit(solution)/shard_map/all_gather | solution.py:151
  54.7 1365.1 %reduce-scatter.2.cloned.1.call-start = ((), (), s32[]{:S(2)}) async-start(), calls=%async_computation.1 | async-start | bytes 8912896 | tf_op jit(solution)/shard_map/reduce_scatter | solution.py:250
  527.9 11.2 collective-permute-start.1
  547.8 33.5 %collective-permute-start.1 = (bf16[16,8192]{1,0:T(8,128)(2,1)}, bf16[16,8192]{1,0:T(8,128)(2,1)}, u32[]{:S(2)}, u32[]{:S(2)}) collective-permute-start(bf16[16,8192]{1,0:T(8,128)(2,1)} %get-tuple-element.1293), channel_id=1, source_target_pairs={{16,0},{32,16},{48,32},{64,48},{80,64},{96,80},{112,96},{128,112},... | collective-permute-start | bytes 786440 | tf_op jit(solution)/shard_map/while/body/eval_jaxpr/ppermute | solution.py:23
  551.6 31.0 %collective-permute-start = (bf16[16,8192]{1,0:T(8,128)(2,1)}, bf16[16,8192]{1,0:T(8,128)(2,1)S(1)}, u32[]{:S(2)}, u32[]{:S(2)}) collective-permute-start(bf16[16,8192]{1,0:T(8,128)(2,1)} %get-tuple-element.1292), channel_id=1, source_target_pairs={{0,16},{16,32},{32,48},{48,64},{64,80},{80,96},{96,112},{112,128},... | collective-permute-start | bytes 786440 | tf_op jit(solution)/shard_map/while/body/eval_jaxpr/ppermute | solution.py:23
  593.2 14.0 collective-permute-start.1
  597.0 11.5 collective-permute-start
  619.1 16.7 %collective-permute-start.1 = (bf16[16,8192]{1,0:T(8,128)(2,1)}, bf16[16,8192]{1,0:T(8,128)(2,1)}, u32[]{:S(2)}, u32[]{:S(2)}) collective-permute-start(bf16[16,8192]{1,0:T(8,128)(2,1)} %get-tuple-element.1293), channel_id=1, source_target_pairs={{16,0},{32,16},{48,32},{64,48},{80,64},{96,80},{112,96},{128,112},... | collective-permute-start | bytes 786440 | tf_op jit(solution)/shard_map/while/body/eval_jaxpr/ppermute | solution.py:23
  622.9 14.1 collective-permute-start
  647.6 14.0 collective-permute-start.1
  651.5 11.5 collective-permute-start
  740.6 10.3 collective-permute-start.3
  765.9 19.4 %collective-permute-start.3 = (bf16[16,8192]{1,0:T(8,128)(2,1)}, bf16[16,8192]{1,0:T(8,128)(2,1)}, u32[]{:S(2)}, u32[]{:S(2)}) collective-permute-start(bf16[16,8192]{1,0:T(8,128)(2,1)} %get-tuple-element.1145), channel_id=1, source_target_pairs={{0,16},{16,32},{32,48},{48,64},{64,80},{80,96},{96,112},{112,128},... | collective-permute-start | bytes 786440 | tf_op jit(solution)/shard_map/while/body/eval_jaxpr/ppermute | solution.py:23
  804.4 15.9 %collective-permute-start.3 = (bf16[16,8192]{1,0:T(8,128)(2,1)}, bf16[16,8192]{1,0:T(8,128)(2,1)}, u32[]{:S(2)}, u32[]{:S(2)}) collective-permute-start(bf16[16,8192]{1,0:T(8,128)(2,1)} %get-tuple-element.1145), channel_id=1, source_target_pairs={{0,16},{16,32},{32,48},{48,64},{64,80},{80,96},{96,112},{112,128},... | collective-permute-start | bytes 786440 | tf_op jit(solution)/shard_map/while/body/eval_jaxpr/ppermute | solution.py:23
  838.7 20.2 %collective-permute-start.3 = (bf16[16,8192]{1,0:T(8,128)(2,1)}, bf16[16,8192]{1,0:T(8,128)(2,1)}, u32[]{:S(2)}, u32[]{:S(2)}) collective-permute-start(bf16[16,8192]{1,0:T(8,128)(2,1)} %get-tuple-element.1145), channel_id=1, source_target_pairs={{0,16},{16,32},{32,48},{48,64},{64,80},{80,96},{96,112},{112,128},... | collective-permute-start | bytes 786440 | tf_op jit(solution)/shard_map/while/body/eval_jaxpr/ppermute | solution.py:23
  877.3 10.6 collective-permute-start.3
  906.3 10.5 collective-permute-start.3
  928.1 17.0 %collective-permute-start.3 = (bf16[16,8192]{1,0:T(8,128)(2,1)}, bf16[16,8192]{1,0:T(8,128)(2,1)}, u32[]{:S(2)}, u32[]{:S(2)}) collective-permute-start(bf16[16,8192]{1,0:T(8,128)(2,1)} %get-tuple-element.1145), channel_id=1, source_target_pairs={{0,16},{16,32},{32,48},{48,64},{64,80},{80,96},{96,112},{112,128},... | collective-permute-start | bytes 786440 | tf_op jit(solution)/shard_map/while/body/eval_jaxpr/ppermute | solution.py:23
  965.0 10.2 collective-permute-start.2
  983.1 12.8 collective-permute-start.3
  1007.9 13.7 collective-permute-start.3
  1057.6 26.8 %collective-permute-start.3 = (bf16[16,8192]{1,0:T(8,128)(2,1)}, bf16[16,8192]{1,0:T(8,128)(2,1)}, u32[]{:S(2)}, u32[]{:S(2)}) collective-permute-start(bf16[16,8192]{1,0:T(8,128)(2,1)} %get-tuple-element.1145), channel_id=1, source_target_pairs={{0,16},{16,32},{32,48},{48,64},{64,80},{80,96},{96,112},{112,128},... | collective-permute-start | bytes 786440 | tf_op jit(solution)/shard_map/while/body/eval_jaxpr/ppermute | solution.py:23
  1096.4 28.5 %collective-permute-start.3 = (bf16[16,8192]{1,0:T(8,128)(2,1)}, bf16[16,8192]{1,0:T(8,128)(2,1)}, u32[]{:S(2)}, u32[]{:S(2)}) collective-permute-start(bf16[16,8192]{1,0:T(8,128)(2,1)} %get-tuple-element.1145), channel_id=1, source_target_pairs={{0,16},{16,32},{32,48},{48,64},{64,80},{80,96},{96,112},{112,128},... | collective-permute-start | bytes 786440 | tf_op jit(solution)/shard_map/while/body/eval_jaxpr/ppermute | solution.py:23
  1137.8 20.6 %collective-permute-start.3 = (bf16[16,8192]{1,0:T(8,128)(2,1)}, bf16[16,8192]{1,0:T(8,128)(2,1)}, u32[]{:S(2)}, u32[]{:S(2)}) collective-permute-start(bf16[16,8192]{1,0:T(8,128)(2,1)} %get-tuple-element.1145), channel_id=1, source_target_pairs={{0,16},{16,32},{32,48},{48,64},{64,80},{80,96},{96,112},{112,128},... | collective-permute-start | bytes 786440 | tf_op jit(solution)/shard_map/while/body/eval_jaxpr/ppermute | solution.py:23
  1169.7 25.2 %collective-permute-start.3 = (bf16[16,8192]{1,0:T(8,128)(2,1)}, bf16[16,8192]{1,0:T(8,128)(2,1)}, u32[]{:S(2)}, u32[]{:S(2)}) collective-permute-start(bf16[16,8192]{1,0:T(8,128)(2,1)} %get-tuple-element.1145), channel_id=1, source_target_pairs={{0,16},{16,32},{32,48},{48,64},{64,80},{80,96},{96,112},{112,128},... | collective-permute-start | bytes 786440 | tf_op jit(solution)/shard_map/while/body/eval_jaxpr/ppermute | solution.py:23
  1206.1 14.5 collective-permute-start.3
  1231.9 14.5 collective-permute-start.3
  1257.6 13.8 collective-permute-start.3
  1263.7 11.8 collective-permute-start.2
  (132 other events, 1181.2 us)
Sparse Core Ops, SparseCore 0:
  10.4 74.3 all-gather.8
  87.1 69.1 all-gather.10
  158.7 68.8 all-gather.12
  229.8 68.6 all-gather.14
  1319.9 99.9 reduce-scatter.1
where the time goes:
time: 1470 us; the launch traced here: 1460 us
  waiting for transfers between devices  546 us (37%)
  starting transfers between devices  377 us (26%)
  local copies, waits for them, and re-layouts  276 us (19%)
  other arithmetic  168 us (11%)
  matrix products  74.3 us (5%)
    ppermute x76, starting transfers between devices, from_behind(): return lax.ppermute(value, axis, pairs)  355 us
    ppermute x76, waiting for transfers between devices, from_behind(): return lax.ppermute(value, axis, pairs)  156 us
    dynamic_update_slice x95, other arithmetic, record(): lax.dynamic_update_index_in_dim(saved_rows, jnp.where(is_valid, update_ro...  134 us
    reduce_scatter x1, waiting for transfers between devices, per_device(): lax.psum_scatter(jnp.concatenate(pieces, axis=1).astype(jnp.bfloat16), 'd...  100 us
    all_gather x1, waiting for transfers between devices, per_device(): lax.all_gather(own_leave[0], 'dp', axis=1, tiled=True)  71.6 us
    all_gather x1, waiting for transfers between devices, per_device(): lax.all_gather(far_enter[0], 'dp', axis=0, tiled=True)  71.3 us
    all_gather x1, waiting for transfers between devices, per_device(): lax.all_gather(far_leave[0], 'dp', axis=1, tiled=True)  70.9 us
    another operation x94, local copies, waits for them, and re-layouts  64 us
  transfers between devices with their start and end apart: 97, of which 60 were waited for; matrix products, arithmetic and copies ran while one was open for 10% of the time, Pallas kernels for 0%

commit v1 on v0

v1 whole, which is shorter than its diff:
```python
import jax
import jax.numpy as jnp
from jax import lax
from jax.experimental import pallas as pl
from jax.experimental.pallas import tpu as pltpu
from jax.sharding import Mesh, PartitionSpec as P

eps_norm = 1e-05
rate = 0.001
beta_one = 0.9
beta_two = 0.95
adam_eps = 1e-08
step_count = 10

LAYERS = 16
RANK = 128
WIDTH = 8192
PARTS = 16
SLICE = WIDTH // PARTS
CHUNK = 128
REACH = LAYERS // 2 + 1
EXTRA = 16

SECTION = ("xh", "y", "c")
DP = ("xl", "z")

BF = jnp.bfloat16
F32 = jnp.float32


def nn(a, b):
    return lax.dot_general(a, b, (((1,), (0,)), ((), ())), preferred_element_type=F32)


def nt(a, b):
    return lax.dot_general(a, b, (((1,), (1,)), ((), ())), preferred_element_type=F32)


def tn(a, b):
    return lax.dot_general(a, b, (((0,), (0,)), ((), ())), preferred_element_type=F32)


def adam_update(weight, moment, second, grad):
    moment_new = beta_one * moment + (1.0 - beta_one) * grad
    second_new = beta_two * second + (1.0 - beta_two) * grad * grad
    corr_one = 1.0 - beta_one**step_count
    corr_two = 1.0 - beta_two**step_count
    weight_new = weight - rate * (moment_new / corr_one) / (
        jnp.sqrt(second_new / corr_two) + adam_eps
    )
    return (weight_new, moment_new, second_new)


def gram_kernel(index_ref, weights_ref, out_ref):
    section = index_ref[0]
    for reach in range(REACH):
        other = lax.rem(section + reach, LAYERS)
        low = jnp.minimum(section, other)
        high = jnp.maximum(section, other)
        block = nt(weights_ref[low, RANK:, :], weights_ref[high]).astype(BF)
        out_ref[2 * reach] = block[:, :RANK]
        out_ref[2 * reach + 1] = block[:, RANK:]


def gram_blocks(section, weights):
    return pl.pallas_call(
        gram_kernel,
        out_shape=jax.ShapeDtypeStruct((2 * REACH, RANK, RANK), BF),
        in_specs=[
            pl.BlockSpec(memory_space=pltpu.SMEM),
            pl.BlockSpec(memory_space=pltpu.VMEM),
        ],
        out_specs=pl.BlockSpec(memory_space=pltpu.VMEM),
        compiler_params=pltpu.CompilerParams(vmem_limit_bytes=32 * 2**20),
        cost_estimate=pl.CostEstimate(
            flops=2 * REACH * RANK * 2 * RANK * SLICE, bytes_accessed=5 * 2**20, transcendentals=0
        ),
    )(section.reshape(1), weights)


def project_kernel(rows_ref, grads_ref, extra_ref, weights_ref, out_ref):
    rows = rows_ref[...]
    grads = grads_ref[...]
    for layer in range(LAYERS):
        out_ref[layer, :CHUNK, : 2 * RANK] = nt(rows, weights_ref[layer]).astype(BF)
        out_ref[layer, :CHUNK, 2 * RANK :] = nt(grads, weights_ref[layer, RANK:, :]).astype(BF)
        out_ref[layer, CHUNK:, :] = extra_ref[...]


def project(rows, grads, extra, weights):
    vmem = pl.BlockSpec(memory_space=pltpu.VMEM)
    return pl.pallas_call(
        project_kernel,
        out_shape=jax.ShapeDtypeStruct((LAYERS, CHUNK + EXTRA, 3 * RANK), BF),
        in_specs=[vmem] * 4,
        out_specs=vmem,
        compiler_params=pltpu.CompilerParams(vmem_limit_bytes=32 * 2**20),
        cost_estimate=pl.CostEstimate(
            flops=2 * CHUNK * SLICE * 3 * RANK * LAYERS, bytes_accessed=6 * 2**20, transcendentals=0
        ),
    )(rows, grads, extra, weights)


def block_place(low, high):
    if high - low < REACH:
        return (low, high - low)
    return (high, LAYERS - (high - low))


def chain_kernel(
    gram_hbm,
    proj_ref,
    square_ref,
    weights_ref,
    rows_ref,
    grads_ref,
    out_ref,
    gram,
    hidden,
    back,
    pre_saved,
    leave_saved,
    rows_saved,
    inv_saved,
    sems,
):
    def fetch(layer):
        for low in range(layer + 1):
            place, reach = block_place(low, layer)
            for half in range(2):
                pltpu.make_async_copy(
                    gram_hbm.at[place, 2 * reach + half],
                    gram.at[
                        pl.ds(low * RANK, RANK), pl.ds((2 * layer + half) * RANK, RANK)
                    ],
                    sems.at[layer],
                ).start()

    def arrived(layer):
        view = gram.at[pl.ds(0, (layer + 1) * RANK), pl.ds(2 * layer * RANK, 2 * RANK)]
        pltpu.make_async_copy(view, view, sems.at[layer]).wait()

    for layer in range(LAYERS):
        fetch(layer)

    square = square_ref[...]
    wide = rows_ref[...].astype(F32)
    for layer in range(LAYERS):
        arrived(layer)
        lanes = slice(2 * layer * RANK, 2 * (layer + 1) * RANK)
        total = proj_ref[layer, :CHUNK, : 2 * RANK].astype(F32)
        if layer > 1:
            before = (layer - 1) * RANK
            total = total + nn(hidden[:, :before], gram[:before, lanes])
        if layer > 0:
            near = slice((layer - 1) * RANK, layer * RANK)
            total = total + nn(hidden[:, near], gram[near, lanes])
        inverse = lax.rsqrt(square * (1.0 / WIDTH) + eps_norm)
        pre_act = total[:, :RANK] * inverse
        act = (pre_act * jax.nn.sigmoid(pre_act)).astype(BF)
        own = slice(layer * RANK, (layer + 1) * RANK)
        hidden[:, own] = act
        pre_saved[layer] = pre_act
        inv_saved[layer] = jnp.broadcast_to(inverse, (CHUNK, RANK))
        self_lanes = slice((2 * layer + 1) * RANK, 2 * (layer + 1) * RANK)
        leave_now = total[:, RANK:]
        leave_next = leave_now + nn(act, gram[own, self_lanes])
        leave_saved[layer] = leave_next
        square = jnp.maximum(
            square
            + jnp.sum(act.astype(F32) * (leave_now + leave_next), axis=1, keepdims=True),
            0.0,
        )
        rows_saved[layer] = wide.astype(BF)
        if layer < LAYERS - 1:
            wide = wide + nn(act, weights_ref[layer, RANK:, :])

    drain = jnp.zeros((CHUNK, 1), F32)
    incoming = grads_ref[...].astype(F32)
    for layer in range(LAYERS - 1, -1, -1):
        own = slice(layer * RANK, (layer + 1) * RANK)
        total = proj_ref[layer, :CHUNK, 2 * RANK :].astype(F32)
        if layer < LAYERS - 2:
            lanes = slice(2 * (layer + 2) * RANK, 2 * LAYERS * RANK)
            total = total + nt(back[:, lanes], gram[own, lanes])
        if layer < LAYERS - 1:
            near = slice(2 * (layer + 1) * RANK, 2 * (layer + 2) * RANK)
            total = total + nt(back[:, near], gram[own, near])
        pre_act = pre_saved[layer]
        inverse = inv_saved[layer]
        hidden_grad = total - drain * leave_saved[layer]
        sig_act = jax.nn.sigmoid(pre_act)
        inner = hidden_grad * (sig_act * (1.0 + pre_act * (1.0 - sig_act)))
        inner = inner.astype(BF).astype(F32)
        unit = (inner * inverse).astype(BF)
        act = hidden[:, own]
        back[:, 2 * layer * RANK : (2 * layer + 1) * RANK] = unit
        back[:, (2 * layer + 1) * RANK : (2 * layer + 2) * RANK] = (
            -drain * act.astype(F32)
        ).astype(BF)
        share = (
            jnp.sum(inner * pre_act, axis=1, keepdims=True)
            * (inverse[:, :1] * inverse[:, :1])
            * (1.0 / WIDTH)
        )
        drain = drain + share
        layer_rows = rows_saved[layer]
        out_ref[layer, :RANK, :] = tn(unit, layer_rows).astype(BF)
        out_ref[layer, RANK:, :] = tn(act, incoming.astype(BF)).astype(BF)
        if layer > 0:
            incoming = (
                incoming
                + nn(unit, weights_ref[layer, :RANK, :])
                - share * layer_rows.astype(F32)
            )


def chain(gram, proj, square, weights, rows, grads):
    vmem = pl.BlockSpec(memory_space=pltpu.VMEM)
    return pl.pallas_call(
        chain_kernel,
        out_shape=jax.ShapeDtypeStruct((LAYERS, 2 * RANK, SLICE), BF),
        in_specs=[pl.BlockSpec(memory_space=pl.ANY)] + [vmem] * 5,
        out_specs=vmem,
        scratch_shapes=[
            pltpu.VMEM((LAYERS * RANK, 2 * LAYERS * RANK), BF),
            pltpu.VMEM((CHUNK, LAYERS * RANK), BF),
            pltpu.VMEM((CHUNK, 2 * LAYERS * RANK), BF),
            pltpu.VMEM((LAYERS, CHUNK, RANK), F32),
            pltpu.VMEM((LAYERS, CHUNK, RANK), F32),
            pltpu.VMEM((LAYERS, CHUNK, SLICE), BF),
            pltpu.VMEM((LAYERS, CHUNK, RANK), F32),
            pltpu.SemaphoreType.DMA((LAYERS,)),
        ],
        compiler_params=pltpu.CompilerParams(vmem_limit_bytes=56 * 2**20),
        cost_estimate=pl.CostEstimate(
            flops=4 * 2**30, bytes_accessed=20 * 2**20, transcendentals=2**20
        ),
    )(gram, proj, square, weights, rows, grads)


def per_device(
    micro_inputs,
    cotangent,
    norm_gain,
    enter_weight,
    enter_moment,
    enter_second,
    leave_weight,
    leave_moment,
    leave_second,
):
    section = lax.axis_index(SECTION)
    part = lax.axis_index(DP)
    gain = lax.dynamic_slice_in_dim(norm_gain[0], part * SLICE, SLICE).astype(F32)

    with jax.named_scope("weights"):
        enter_half = enter_weight[0].astype(BF).astype(F32)
        scaled = (enter_half * gain[:, None]).astype(BF)
        own = jnp.concatenate([scaled.T, leave_weight[0].astype(BF)], axis=0)
        weights = lax.all_gather(own, SECTION, axis=0, tiled=False)

    with jax.named_scope("rows"):
        own_rows = CHUNK // PARTS
        both = jnp.stack(
            [
                lax.dynamic_slice_in_dim(
                    value.reshape(CHUNK, WIDTH), section * own_rows, own_rows, 0
                )
                for value in (micro_inputs, cotangent)
            ]
        )
        both = both.reshape(2 * own_rows, PARTS, SLICE).transpose(1, 0, 2)
        both = lax.all_to_all(both, DP, split_axis=0, concat_axis=0, tiled=True)
        both = both.reshape(PARTS, 2, own_rows, SLICE)
        rows = both[:, 0].reshape(CHUNK, SLICE)
        grads = both[:, 1].reshape(CHUNK, SLICE)

    with jax.named_scope("gram"):
        blocks = gram_blocks(section, weights)
        pieces = blocks.reshape(PARTS, 2 * REACH * RANK // PARTS, RANK)
        pieces = lax.all_to_all(pieces, DP, split_axis=0, concat_axis=0, tiled=True)
        piece = jnp.sum(pieces.astype(F32), axis=0).astype(BF)
        spread = jnp.broadcast_to(piece[None], pieces.shape)
        blocks = lax.all_to_all(spread, DP, split_axis=0, concat_axis=0, tiled=True)
        blocks = blocks.reshape(2 * REACH, RANK, RANK)
        gram = lax.all_gather(blocks, SECTION, axis=0, tiled=False)

    with jax.named_scope("project"):
        wide = rows.astype(F32)
        square = jnp.sum(wide * wide, axis=1)
        high = square.astype(BF)
        low = (square - high.astype(F32)).astype(BF)
        extra = jnp.zeros((EXTRA, 3 * RANK), BF)
        extra = extra.at[0, :CHUNK].set(high).at[1, :CHUNK].set(low)
        proj = project(rows, grads, extra, weights)
        proj = lax.all_to_all(proj, DP, split_axis=0, concat_axis=0, tiled=True)
        proj = jnp.sum(proj.astype(F32), axis=0)
        square = proj[CHUNK, :CHUNK] + proj[CHUNK + 1, :CHUNK]
        proj = jnp.broadcast_to(proj.astype(BF)[None], (PARTS,) + proj.shape)
        proj = lax.all_to_all(proj, DP, split_axis=0, concat_axis=0, tiled=True)

    with jax.named_scope("chain"):
        shares = chain(gram, proj, square[:, None], weights, rows, grads)

    with jax.named_scope("sum"):
        shares = lax.all_to_all(shares, SECTION, split_axis=0, concat_axis=0, tiled=True)
        total = jnp.sum(shares.astype(F32), axis=0)

    with jax.named_scope("adam"):
        enter_grad = total[:RANK].T * gain[:, None]
        leave_grad = total[RANK:]
        new_enter = adam_update(enter_weight[0], enter_moment[0], enter_second[0], enter_grad)
        new_leave = adam_update(leave_weight[0], leave_moment[0], leave_second[0], leave_grad)
    return tuple(value[None] for value in new_enter + new_leave)


def solution(mesh):
    split = Mesh(mesh.devices.reshape(2, 4, 2, 2, 8), SECTION + DP)
    rows = P(None, None, DP, None)
    enter = P(SECTION, DP, None)
    leave = P(SECTION, None, DP)
    return jax.shard_map(
        per_device,
        mesh=split,
        in_specs=(rows, rows, P(SECTION, None)) + (enter,) * 3 + (leave,) * 3,
        out_specs=(enter,) * 3 + (leave,) * 3,
        check_vma=False,
    )
```

time: 1470 us -> 341 us (0.23)
  waiting for transfers between devices: 546 us -> 162 us
  starting transfers between devices: 377 us -> 10.3 us
  local copies, waits for them, and re-layouts: 276 us -> 13.3 us
  other arithmetic: 168 us -> 6.97 us
  blocking collectives: 0 us -> 106 us
  matrix products: 74.3 us -> 0 us
  Pallas kernels: 0 us -> 25.2 us
    ppermute x92 -> x0, starting transfers between devices: 377 us -> none  [the longest x76 355 us: from_behind(): return lax.ppermute(value, axis, pairs)]
    ppermute x92 -> x0, waiting for transfers between devices: 218 us -> none  [the longest x76 156 us: from_behind(): return lax.ppermute(value, axis, pairs)]
    all_gather x4 -> x2, waiting for transfers between devices: 227 us -> 62.5 us  [the longest x1 62.5 us: per_device(): weights = lax.all_gather(own, SECTION, axis=0, tiled=False)]
    dynamic_update_slice x95 -> x0, other arithmetic: 134 us -> none  [record(): lax.dynamic_update_index_in_dim(saved_rows, jnp.where(is_valid, update_ro...]
    slice x39 -> x0, local copies, waits for them, and re-layouts: 116 us -> none  [the longest x19 58.1 us: forward_tick(): micro_inputs[1]]
    all_to_all x0 -> x4, blocking collectives: none -> 106 us  [the longest x1 45.8 us: per_device(): proj = lax.all_to_all(proj, DP, split_axis=0, concat_axis=0, tiled=True)]
    reduce_scatter x1 -> x0, waiting for transfers between devices: 100 us -> none  [per_device(): lax.psum_scatter(jnp.concatenate(pieces, axis=1).astype(jnp.bfloat16), 'd...]
    all_to_all x0 -> x2, waiting for transfers between devices: none -> 99.6 us  [the longest x1 59.4 us: per_device(): lax.all_to_all(shares, SECTION, split_axis=0, concat_axis=0, tiled=True)]
  transfers between devices with their start and end apart: 97 -> 4, of which waited for: 60 -> 3; matrix products, arithmetic and copies ran while one was open for 10% -> 1% of each run, Pallas kernels for 0% -> 1%
where the time goes in v1:
time: 341 us; the launch traced here: 338 us
  waiting for transfers between devices  162 us (48%)
  blocking collectives  106 us (31%)
  Pallas kernels  25.2 us (7%)
  between operations  14.3 us (4%)
  local copies, waits for them, and re-layouts  13.3 us (4%)
  starting transfers between devices  10.3 us (3%)
  other arithmetic  6.97 us (2%)
    all_gather x1, waiting for transfers between devices, per_device(): weights = lax.all_gather(own, SECTION, axis=0, tiled=False)  62.5 us
    all_to_all x1, waiting for transfers between devices, per_device(): lax.all_to_all(shares, SECTION, split_axis=0, concat_axis=0, tiled=True)  59.4 us
    all_to_all x1, blocking collectives, per_device(): proj = lax.all_to_all(proj, DP, split_axis=0, concat_axis=0, tiled=True)  45.8 us
    all_to_all x1, waiting for transfers between devices, per_device(): proj = lax.all_to_all(proj, DP, split_axis=0, concat_axis=0, tiled=True)  40.2 us
    all_to_all x1, blocking collectives, per_device(): pieces = lax.all_to_all(pieces, DP, split_axis=0, concat_axis=0, tiled=True)  26.4 us
    pallas_call x1, Pallas kernels, chain(): pl.pallas_call(chain_kernel, out_shape=jax.ShapeDtypeStruct((LAYERS, 2 *...  22.4 us
    all_to_all x1, blocking collectives, per_device(): blocks = lax.all_to_all(spread, DP, split_axis=0, concat_axis=0, tiled=True)  21.8 us
    all_to_all x1, blocking collectives, per_device(): both = lax.all_to_all(both, DP, split_axis=0, concat_axis=0, tiled=True)  12 us
  transfers between devices with their start and end apart: 4, of which 3 were waited for; matrix products, arithmetic and copies ran while one was open for 1% of the time, Pallas kernels for 1%

profile of v1, /device:TPU:8, one launch (start us, length us, event | category | flops | bytes accessed | tf_op | source)
XLA Modules:
  0.0 338.1 jit_solution(6589727260758241980)
XLA Ops:
  7.2 1.1 copy.36
  8.3 1.0 bitcast_convert_fusion
  9.3 0.7 dynamic-slice_convert_fusion
  10.0 0.7 pad_maximum_fusion
  10.8 62.5 %all-gather.6.cloned.1.call-done = bf16[4096,512]{1,0:T(8,128)(2,1)} async-done(((bf16[256,512]{1,0:T(8,128)(2,1)}), bf16[4096,512]{1,0:T(8,128)(2,1)}) %all-gather.6.cloned.1.call-update) | async-done | bytes 4194320 | tf_op jit(solution)/shard_map/weights/all_gather | solution.py:261
  73.3 2.2 copy-done
  75.5 0.9 gram.1
  76.3 26.4 %all_to_all.30 = bf16[16,144,128]{2,1,0:T(8,128)(2,1)S(1)} all-to-all(bf16[16,144,128]{2,1,0:T(8,128)(2,1)S(1)} %bitcast.73), channel_id=1, replica_groups=mesh['xh'=2,'y'=4,'c'=2,'xl'=2,'z'=8] {'xl','z'}, dimensions={0} | all-to-all | bytes 1179648 | tf_op jit(solution)/shard_map/gram/all_to_all | solution.py:282
  102.9 21.8 %all_to_all.31 = bf16[16,144,128]{2,1,0:T(8,128)(2,1)} all-to-all(bf16[16,144,128]{2,1,0:T(8,128)(2,1)S(1)} %broadcast_in_dim.16), channel_id=1, replica_groups=mesh['xh'=2,'y'=4,'c'=2,'xl'=2,'z'=8] {'xl','z'}, dimensions={0} | all-to-all | bytes 1179648 | tf_op jit(solution)/shard_map/gram/all_to_all | solution.py:285
  124.7 1.0 dynamic-slice_bitcast_fusion
  125.9 0.2 copy.38
  126.0 12.0 %all_to_all.32 = bf16[16,16,512]{2,1,0:T(8,128)(2,1)S(1)} all-to-all(bf16[16,16,512]{2,1,0:T(8,128)(2,1)S(1)} %copy.38), channel_id=1, replica_groups=mesh['xh'=2,'y'=4,'c'=2,'xl'=2,'z'=8] {'xl','z'}, dimensions={0} | all-to-all | bytes 524288 | tf_op jit(solution)/shard_map/rows/all_to_all | solution.py:274
  138.3 0.2 scatter.9.extra_ref
  138.5 2.3 copy-done.1
  140.8 1.9 project.1
  142.7 45.8 %all_to_all.33 = bf16[16,144,384]{2,1,0:T(8,128)(2,1)S(1)} all-to-all(bf16[16,144,384]{2,1,0:T(8,128)(2,1)S(1)} %project.1), channel_id=1, replica_groups=mesh['xh'=2,'y'=4,'c'=2,'xl'=2,'z'=8] {'xl','z'}, dimensions={0} | all-to-all | bytes 3538944 | tf_op jit(solution)/shard_map/project/all_to_all | solution.py:297
  188.5 0.2 convert_reduce_fusion.1
  188.8 1.4 broadcast_in_dim.17
  190.1 3.9 %all-to-all-start.4 = ((bf16[16,144,384]{2,1,0:T(8,128)(2,1)}), bf16[16,144,384]{2,1,0:T(8,128)(2,1)S(1)}, u32[]{:S(2)}, u32[]{:S(2)}) async-start(bf16[16,144,384]{2,1,0:T(8,128)(2,1)} %broadcast_in_dim.17), calls=%async_computation.4 | async-start | bytes 3538944 | tf_op jit(solution)/shard_map/project/all_to_all | solution.py:301
  194.1 0.7 copy.39.square_ref
  194.8 40.2 %all-to-all-done.4.proj_ref = bf16[16,144,384]{2,1,0:T(8,128)(2,1)S(1)} async-done(((bf16[16,144,384]{2,1,0:T(8,128)(2,1)}), bf16[16,144,384]{2,1,0:T(8,128)(2,1)S(1)}, u32[]{:S(2)}, u32[]{:S(2)}) %all-to-all-start.4) | async-done | bytes 1769504 | tf_op jit(solution)/shard_map/project/all_to_all | solution.py:301
  235.0 1.2 copy-done.4
  236.2 22.4 %chain.1 = bf16[16,256,512]{2,1,0:T(8,128)(2,1)} custom-call(bf16[16,18,128,128]{3,2,1,0:T(8,128)(2,1)} %all-gather.4.cloned.1.call-done.gram_hbm, bf16[16,144,384]{2,1,0:T(8,128)(2,1)} %copy-done.4, f32[128,1]{1,0:T(8,128)} %copy.39.square_ref, bf16[16,256,512]{2,1,0:T(8,128)(2,1)} %bitcast.70, bf16[128,512]{1,0:T(8,128)(2,1)} %copy-done.3, ...), custom_call_target="tpu_custom_call" | custom-call | flops 4294967296 | bytes 20971520 | tf_op jit(solution)/shard_map/chain/pallas_call | solution.py:220
  258.7 6.3 %all-to-all-start.5 = ((bf16[16,256,512]{2,1,0:T(8,128)(2,1)}), bf16[16,256,512]{2,1,0:T(8,128)(2,1)}, u32[]{:S(2)}, u32[]{:S(2)}) async-start(bf16[16,256,512]{2,1,0:T(8,128)(2,1)} %chain.1), calls=%async_computation.5 | async-start | bytes 8388608 | tf_op jit(solution)/shard_map/sum/all_to_all | solution.py:307
  265.0 0.1 copy.37
  265.3 59.4 %all-to-all-done.5 = bf16[16,256,512]{2,1,0:T(8,128)(2,1)} async-done(((bf16[16,256,512]{2,1,0:T(8,128)(2,1)}), bf16[16,256,512]{2,1,0:T(8,128)(2,1)}, u32[]{:S(2)}, u32[]{:S(2)}) %all-to-all-start.5) | async-done | bytes 4194336 | tf_op jit(solution)/shard_map/sum/all_to_all | solution.py:307
  324.7 2.8 convert_reduce_fusion
  327.5 0.2 bitcast_subtract_fusion.1
  327.7 0.8 copy.41
  328.6 0.8 copy.42
  329.4 0.8 copy.43
  330.3 1.0 fusion.6
  (35 shorter events, 0.8 us)
Async XLA Ops:
  7.2 66.1 %all-gather.6.cloned.1.call-start = ((), (), s32[]{:S(2)}) async-start(), calls=%async_computation.7 | async-start | bytes 4456448 | tf_op jit(solution)/shard_map/weights/all_gather | solution.py:261
  10.7 224.3 %all-gather.4.cloned.1.call-start = ((), (), s32[]{:S(2)}) async-start(), calls=%async_computation.6 | async-start | bytes 10027008 | tf_op jit(solution)/shard_map/gram/all_gather | solution.py:287
  73.3 2.2 copy-start
  138.5 4.2 %copy-start.2 = (bf16[128,512]{1,0:T(8,128)(2,1)}, bf16[128,512]{1,0:T(8,128)(2,1)S(1)}, u32[]{:S(2)}) copy-start(bf16[128,512]{1,0:T(8,128)(2,1)S(1)} %get-tuple-element.48.grads_ref) | copy-start | bytes 393220
  138.5 4.2 %copy-start.3 = (bf16[128,512]{1,0:T(8,128)(2,1)}, bf16[128,512]{1,0:T(8,128)(2,1)S(1)}, u32[]{:S(2)}) copy-start(bf16[128,512]{1,0:T(8,128)(2,1)S(1)} %get-tuple-element.49.rows_ref) | copy-start | bytes 393220
  138.5 2.3 copy-start.1
  190.1 44.9 %all-to-all-start.4 = ((bf16[16,144,384]{2,1,0:T(8,128)(2,1)}), bf16[16,144,384]{2,1,0:T(8,128)(2,1)S(1)}, u32[]{:S(2)}, u32[]{:S(2)}) async-start(bf16[16,144,384]{2,1,0:T(8,128)(2,1)} %broadcast_in_dim.17), calls=%async_computation.4 | async-start | bytes 3538944 | tf_op jit(solution)/shard_map/project/all_to_all | solution.py:301
  235.0 1.2 copy-start.4
  258.7 6.3 %copy-start.8 = (f32[1,512,128]{2,1,0:T(8,128)S(1)}, f32[1,512,128]{2,1,0:T(8,128)}, u32[]{:S(2)}) copy-start(f32[1,512,128]{2,1,0:T(8,128)} %param.17) | copy-start | bytes 786436
  258.7 6.4 %copy-start.9 = (f32[1,512,128]{2,1,0:T(8,128)S(1)}, f32[1,512,128]{2,1,0:T(8,128)}, u32[]{:S(2)}) copy-start(f32[1,512,128]{2,1,0:T(8,128)} %param.18) | copy-start | bytes 786436
  258.7 66.0 %all-to-all-start.5 = ((bf16[16,256,512]{2,1,0:T(8,128)(2,1)}), bf16[16,256,512]{2,1,0:T(8,128)(2,1)}, u32[]{:S(2)}, u32[]{:S(2)}) async-start(bf16[16,256,512]{2,1,0:T(8,128)(2,1)} %chain.1), calls=%async_computation.5 | async-start | bytes 8388608 | tf_op jit(solution)/shard_map/sum/all_to_all | solution.py:307
  327.5 2.8 copy-start.5
  327.5 2.7 copy-start.6
  327.5 2.7 copy-start.7
Sparse Core Ops, SparseCore 0:
  11.3 61.8 all-gather.5
  124.9 94.2 all-gather.3

commit v2 on v1

v2 whole, which is shorter than its diff:
```python
import jax
import jax.numpy as jnp
from jax import lax
from jax.experimental import pallas as pl
from jax.experimental.pallas import tpu as pltpu
from jax.sharding import Mesh, PartitionSpec as P

eps_norm = 1e-05
rate = 0.001
beta_one = 0.9
beta_two = 0.95
adam_eps = 1e-08
step_count = 10

LAYERS = 16
RANK = 128
WIDTH = 8192
PARTS = 16
SLICE = WIDTH // PARTS
CHUNK = 128
OWN_ROWS = CHUNK // PARTS
HALF = LAYERS // 2
PACKED = RANK + 4 * 2 * OWN_ROWS + 2 * OWN_ROWS

SECTION = ("xh", "y", "c")
DP = ("xl", "z")

BF = jnp.bfloat16
F32 = jnp.float32


def nn(a, b):
    return lax.dot_general(a, b, (((1,), (0,)), ((), ())), preferred_element_type=F32)


def nt(a, b):
    return lax.dot_general(a, b, (((1,), (1,)), ((), ())), preferred_element_type=F32)


def tn(a, b):
    return lax.dot_general(a, b, (((0,), (0,)), ((), ())), preferred_element_type=F32)


VMEM = pl.BlockSpec(memory_space=pltpu.VMEM)
SMEM = pl.BlockSpec(memory_space=pltpu.SMEM)
ANY = pl.BlockSpec(memory_space=pl.ANY)


def params(mebibytes):
    return pltpu.CompilerParams(vmem_limit_bytes=mebibytes * 2**20)


def cost(flops, bytes_accessed):
    return pl.CostEstimate(flops=flops, bytes_accessed=bytes_accessed, transcendentals=0)


def own_kernel(enter_ref, leave_ref, gain_ref, out_ref):
    enter = enter_ref[0].astype(BF).astype(F32).T * gain_ref[...]
    enter = enter.astype(BF)
    leave = leave_ref[0].astype(BF)
    for copy in range(HALF):
        out_ref[copy, :RANK, :] = enter
        out_ref[copy, RANK:, :] = leave


def own_weights(enter_weight, leave_weight, gain):
    return pl.pallas_call(
        own_kernel,
        out_shape=jax.ShapeDtypeStruct((HALF, 2 * RANK, SLICE), BF),
        in_specs=[VMEM] * 3,
        out_specs=VMEM,
        compiler_params=params(16),
        cost_estimate=cost(2**18, 3 * 2**20),
    )(enter_weight, leave_weight, gain)


def load_weights(core, near_ref, far_ref, weights, sems):
    copies = [
        pltpu.make_async_copy(near_ref, weights.at[core], sems.at[0]),
        pltpu.make_async_copy(far_ref, weights.at[1 - core], sems.at[1]),
    ]
    for copy in copies:
        copy.start()
    return copies


def gram_kernel(index_ref, near_ref, far_ref, both_ref, out_ref, weights, sems):
    section = index_ref[0]
    copies = load_weights(index_ref[1], near_ref, far_ref, weights, sems)
    both = both_ref[...]
    for part in range(PARTS):
        for lane in range(SLICE // 128):
            first = RANK + 2 * OWN_ROWS * lane
            start = SLICE * part + 128 * lane
            out_ref[part, first : first + 2 * OWN_ROWS, :] = both[:, start : start + 128]
    wide = both.astype(F32)[:OWN_ROWS]
    square = jnp.sum(wide * wide, axis=1, keepdims=True)
    high = square.astype(BF).astype(F32)
    tail = jnp.concatenate(
        [
            jnp.broadcast_to(high, (OWN_ROWS, RANK)),
            jnp.broadcast_to(square - high, (OWN_ROWS, RANK)),
        ],
        axis=0,
    ).astype(BF)
    for part in range(PARTS):
        out_ref[part, PACKED - 2 * OWN_ROWS :, :] = tail
    for copy in copies:
        copy.wait()

    def layer_rows(layer, rows):
        return weights[lax.rem(layer, 2), layer // 2, rows, :]

    leave = pl.ds(RANK, RANK)
    out_ref[0, :RANK, :] = nt(layer_rows(section, leave), layer_rows(section, leave)).astype(BF)
    for reach in range(1, HALF + 1):
        other = lax.rem(section + reach, LAYERS)
        low = jnp.minimum(section, other)
        high = jnp.maximum(section, other)
        if reach < HALF:
            block = nt(layer_rows(low, leave), layer_rows(high, pl.ds(0, 2 * RANK))).astype(BF)
            out_ref[2 * reach - 1, :RANK, :] = block[:, :RANK]
            out_ref[2 * reach, :RANK, :] = block[:, RANK:]
        else:
            start = pl.multiple_of((section // HALF) * RANK, RANK)
            block = nt(layer_rows(low, leave), layer_rows(high, pl.ds(start, RANK)))
            out_ref[2 * reach - 1, :RANK, :] = block.astype(BF)


def gram_and_rows(index, near, far, both):
    return pl.pallas_call(
        gram_kernel,
        out_shape=jax.ShapeDtypeStruct((PARTS, PACKED, RANK), BF),
        in_specs=[SMEM, ANY, ANY, VMEM],
        out_specs=VMEM,
        scratch_shapes=[
            pltpu.VMEM((2, HALF, 2 * RANK, SLICE), BF),
            pltpu.SemaphoreType.DMA((2,)),
        ],
        compiler_params=params(32),
        cost_estimate=cost(2 * LAYERS * RANK * RANK * SLICE, 6 * 2**20),
    )(index, near, far, both)


def block_place(low, high, half):
    reach = high - low
    if reach == 0:
        return (low, 0)
    if reach < HALF:
        return (low, 2 * reach - 1 + half)
    if reach == HALF:
        return ((low, high)[half], LAYERS - 1)
    return (high, 2 * (LAYERS - reach) - 1 + half)


def project_kernel(
    index_ref, packed_ref, near_ref, far_ref, out_ref, rows_ref, grads_ref, square_ref, weights, sems
):
    copies = load_weights(index_ref[1], near_ref, far_ref, weights, sems)
    lanes = []
    for lane in range(SLICE // 128):
        first = RANK + 2 * OWN_ROWS * lane
        lanes.append(packed_ref[:, first : first + 2 * OWN_ROWS, :].astype(F32))
    both = jnp.concatenate(lanes, axis=2)
    rows = both[:, :OWN_ROWS, :].reshape(CHUNK, SLICE).astype(BF)
    grads = both[:, OWN_ROWS:, :].reshape(CHUNK, SLICE).astype(BF)
    rows_ref[...] = rows
    grads_ref[...] = grads
    tail = packed_ref[:, PACKED - 2 * OWN_ROWS :, :].astype(F32)
    square_ref[...] = (tail[:, :OWN_ROWS, :] + tail[:, OWN_ROWS:, :]).reshape(CHUNK, RANK)
    for copy in copies:
        copy.wait()
    for layer in range(LAYERS):
        place = (layer % 2, layer // 2)
        out_ref[layer, :, : 2 * RANK] = nt(rows, weights[place]).astype(BF)
        out_ref[layer, :, 2 * RANK :] = nt(grads, weights[place][RANK:, :]).astype(BF)


def project(index, packed, near, far):
    return pl.pallas_call(
        project_kernel,
        out_shape=(
            jax.ShapeDtypeStruct((LAYERS, CHUNK, 3 * RANK), BF),
            jax.ShapeDtypeStruct((CHUNK, SLICE), BF),
            jax.ShapeDtypeStruct((CHUNK, SLICE), BF),
            jax.ShapeDtypeStruct((CHUNK, RANK), F32),
        ),
        in_specs=[SMEM, VMEM, ANY, ANY],
        out_specs=(VMEM,) * 4,
        scratch_shapes=[
            pltpu.VMEM((2, HALF, 2 * RANK, SLICE), BF),
            pltpu.SemaphoreType.DMA((2,)),
        ],
        compiler_params=params(32),
        cost_estimate=cost(2 * CHUNK * SLICE * 3 * RANK * LAYERS, 7 * 2**20),
    )(index, packed, near, far)


def chain_kernel(
    index_ref,
    gram_hbm,
    proj_ref,
    square_ref,
    near_ref,
    far_ref,
    rows_ref,
    grads_ref,
    keep_ref,
    pass_ref,
    gram,
    weights,
    shares,
    hidden,
    back,
    pre_saved,
    leave_saved,
    rows_saved,
    inv_saved,
    gram_sems,
    sems,
    out_sems,
):
    core = index_ref[1]
    copies = load_weights(core, near_ref, far_ref, weights, sems)

    def fetch(layer):
        for low in range(layer + 1):
            for half in range(2):
                if low == layer and half == 0:
                    continue
                place, slot = block_place(low, layer, half)
                pltpu.make_async_copy(
                    gram_hbm.at[place, slot],
                    gram.at[
                        pl.ds(low * RANK, RANK), pl.ds((2 * layer + half) * RANK, RANK)
                    ],
                    gram_sems.at[layer],
                ).start()

    def arrived(layer):
        view = gram.at[pl.ds(0, (2 * layer + 1) * (RANK // 2)), pl.ds(0, 2 * RANK)]
        pltpu.make_async_copy(view, view, gram_sems.at[layer]).wait()

    for layer in range(LAYERS):
        fetch(layer)
    for copy in copies:
        copy.wait()

    square = square_ref[...][:, :1]
    wide = rows_ref[...].astype(F32)
    for layer in range(LAYERS):
        arrived(layer)
        lanes = slice(2 * layer * RANK, 2 * (layer + 1) * RANK)
        total = proj_ref[layer, :, : 2 * RANK].astype(F32)
        if layer > 1:
            before = (layer - 1) * RANK
            total = total + nn(hidden[:, :before], gram[:before, lanes])
        if layer > 0:
            near = slice((layer - 1) * RANK, layer * RANK)
            total = total + nn(hidden[:, near], gram[near, lanes])
        inverse = lax.rsqrt(square * (1.0 / WIDTH) + eps_norm)
        pre_act = total[:, :RANK] * inverse
        act = (pre_act * jax.nn.sigmoid(pre_act)).astype(BF)
        own = slice(layer * RANK, (layer + 1) * RANK)
        hidden[:, own] = act
        pre_saved[layer] = pre_act
        inv_saved[layer] = jnp.broadcast_to(inverse, (CHUNK, RANK))
        self_lanes = slice((2 * layer + 1) * RANK, 2 * (layer + 1) * RANK)
        leave_now = total[:, RANK:]
        leave_next = leave_now + nn(act, gram[own, self_lanes])
        leave_saved[layer] = leave_next
        square = jnp.maximum(
            square
            + jnp.sum(act.astype(F32) * (leave_now + leave_next), axis=1, keepdims=True),
            0.0,
        )
        rows_saved[layer] = wide.astype(BF)
        if layer < LAYERS - 1:
            wide = wide + nn(act, weights[layer % 2, layer // 2, RANK:, :])

    drain = jnp.zeros((CHUNK, 1), F32)
    incoming = grads_ref[...].astype(F32)
    for layer in range(LAYERS - 1, -1, -1):
        own = slice(layer * RANK, (layer + 1) * RANK)
        total = proj_ref[layer, :, 2 * RANK :].astype(F32)
        if layer < LAYERS - 2:
            lanes = slice(2 * (layer + 2) * RANK, 2 * LAYERS * RANK)
            total = total + nt(back[:, lanes], gram[own, lanes])
        if layer < LAYERS - 1:
            near = slice(2 * (layer + 1) * RANK, 2 * (layer + 2) * RANK)
            total = total + nt(back[:, near], gram[own, near])
        pre_act = pre_saved[layer]
        inverse = inv_saved[layer]
        hidden_grad = total - drain * leave_saved[layer]
        sig_act = jax.nn.sigmoid(pre_act)
        inner = hidden_grad * (sig_act * (1.0 + pre_act * (1.0 - sig_act)))
        inner = inner.astype(BF).astype(F32)
        unit = (inner * inverse).astype(BF)
        act = hidden[:, own]
        back[:, 2 * layer * RANK : (2 * layer + 1) * RANK] = unit
        back[:, (2 * layer + 1) * RANK : (2 * layer + 2) * RANK] = (
            -drain * act.astype(F32)
        ).astype(BF)
        share = (
            jnp.sum(inner * pre_act, axis=1, keepdims=True)
            * (inverse[:, :1] * inverse[:, :1])
            * (1.0 / WIDTH)
        )
        drain = drain + share
        layer_rows = rows_saved[layer]
        side = core if layer % 2 == 0 else 1 - core
        shares[side, layer // 2, :RANK, :] = tn(unit, layer_rows).astype(BF)
        shares[side, layer // 2, RANK:, :] = tn(act, incoming.astype(BF)).astype(BF)
        if layer > 0:
            incoming = (
                incoming
                + nn(unit, weights[layer % 2, layer // 2, :RANK, :])
                - share * layer_rows.astype(F32)
            )
    last = [
        pltpu.make_async_copy(shares.at[0], keep_ref, out_sems.at[0]),
        pltpu.make_async_copy(shares.at[1], pass_ref, out_sems.at[1]),
    ]
    for copy in last:
        copy.start()
    for copy in last:
        copy.wait()


def chain(index, gram, proj, square, near, far, rows, grads):
    side = jax.ShapeDtypeStruct((HALF, 2 * RANK, SLICE), BF)
    return pl.pallas_call(
        chain_kernel,
        out_shape=(side, side),
        in_specs=[SMEM, ANY, VMEM, VMEM, ANY, ANY, VMEM, VMEM],
        out_specs=(ANY, ANY),
        scratch_shapes=[
            pltpu.VMEM((LAYERS * RANK, 2 * LAYERS * RANK), BF),
            pltpu.VMEM((2, HALF, 2 * RANK, SLICE), BF),
            pltpu.VMEM((2, HALF, 2 * RANK, SLICE), BF),
            pltpu.VMEM((CHUNK, LAYERS * RANK), BF),
            pltpu.VMEM((CHUNK, 2 * LAYERS * RANK), BF),
            pltpu.VMEM((LAYERS, CHUNK, RANK), F32),
            pltpu.VMEM((LAYERS, CHUNK, RANK), F32),
            pltpu.VMEM((LAYERS, CHUNK, SLICE), BF),
            pltpu.VMEM((LAYERS, CHUNK, RANK), F32),
            pltpu.SemaphoreType.DMA((LAYERS,)),
            pltpu.SemaphoreType.DMA((2,)),
            pltpu.SemaphoreType.DMA((2,)),
        ],
        compiler_params=params(56),
        cost_estimate=cost(4 * 2**30, 20 * 2**20),
    )(index, gram, proj, square, near, far, rows, grads)


def adam_update(weight, moment, second, grad):
    moment_new = beta_one * moment + (1.0 - beta_one) * grad
    second_new = beta_two * second + (1.0 - beta_two) * grad * grad
    corr_one = 1.0 - beta_one**step_count
    corr_two = 1.0 - beta_two**step_count
    weight_new = weight - rate * (moment_new / corr_one) / (
        jnp.sqrt(second_new / corr_two) + adam_eps
    )
    return (weight_new, moment_new, second_new)


def adam_kernel(parts_ref, gain_ref, *refs):
    ins, outs = refs[:6], refs[6:]
    total = jnp.sum(parts_ref[...].astype(F32), axis=0)
    grads = ((total[:RANK] * gain_ref[...]).T, total[RANK:])
    for first, grad in zip((0, 3), grads):
        updated = adam_update(*(ref[0] for ref in ins[first : first + 3]), grad)
        for ref, value in zip(outs[first : first + 3], updated):
            ref[0] = value


def adam(parts, gain, state):
    return pl.pallas_call(
        adam_kernel,
        out_shape=tuple(jax.ShapeDtypeStruct(value.shape, F32) for value in state),
        in_specs=[VMEM] * 8,
        out_specs=(VMEM,) * 6,
        compiler_params=params(32),
        cost_estimate=cost(2**22, 5 * 2**20),
    )(parts, gain, *state)


def per_device(
    micro_inputs,
    cotangent,
    norm_gain,
    enter_weight,
    enter_moment,
    enter_second,
    leave_weight,
    leave_moment,
    leave_second,
):
    section = lax.axis_index(SECTION)
    part = lax.axis_index(DP)
    core = lax.axis_index("c")
    index = jnp.stack([section, core])
    gain = lax.dynamic_slice_in_dim(norm_gain, part * SLICE, SLICE, axis=1).astype(F32)
    cores = [(0, 1), (1, 0)]

    def exchange(value, axes):
        return lax.all_to_all(value, axes, split_axis=0, concat_axis=0, tiled=True)

    def spread(value):
        return exchange(jnp.broadcast_to(value[None], (PARTS,) + value.shape), DP)

    with jax.named_scope("weights"):
        near = exchange(own_weights(enter_weight, leave_weight, gain), ("xh", "y"))
        far = lax.ppermute(near, "c", cores)

    with jax.named_scope("gram"):
        both = jnp.concatenate(
            [
                lax.dynamic_slice_in_dim(
                    value.reshape(CHUNK, WIDTH), section * OWN_ROWS, OWN_ROWS, 0
                )
                for value in (micro_inputs, cotangent)
            ]
        )
        packed = exchange(gram_and_rows(index, near, far, both), DP)
        blocks = spread(jnp.sum(packed[:, :RANK, :].astype(F32), axis=0).astype(BF))
        gram = lax.all_gather(blocks, SECTION, axis=0, tiled=False)

    with jax.named_scope("project"):
        proj, rows, grads, square = project(index, packed, near, far)
        proj = spread(jnp.sum(exchange(proj, DP).astype(F32), axis=0).astype(BF))

    with jax.named_scope("chain"):
        keep, other = chain(index, gram, proj, square, near, far, rows, grads)

    with jax.named_scope("sum"):
        received = lax.ppermute(other, "c", cores)
        parts = exchange((keep.astype(F32) + received.astype(F32)).astype(BF), ("xh", "y"))

    with jax.named_scope("adam"):
        return adam(
            parts,
            gain,
            (enter_weight, enter_moment, enter_second, leave_weight, leave_moment, leave_second),
        )


def solution(mesh):
    split = Mesh(mesh.devices.reshape(2, 4, 2, 2, 8), SECTION + DP)
    rows = P(None, None, DP, None)
    enter = P(SECTION, DP, None)
    leave = P(SECTION, None, DP)
    return jax.shard_map(
        per_device,
        mesh=split,
        in_specs=(rows, rows, P(SECTION, None)) + (enter,) * 3 + (leave,) * 3,
        out_specs=(enter,) * 3 + (leave,) * 3,
        check_vma=False,
    )
```

time: 341 us -> 273 us (0.80)
  waiting for transfers between devices: 162 us -> 14.3 us
  blocking collectives: 106 us -> 199 us
  starting transfers between devices: 10.3 us -> 0.38 us
  Pallas kernels: 25.2 us -> 34.3 us
  local copies, waits for them, and re-layouts: 13.3 us -> 5.46 us
  other arithmetic: 6.97 us -> 3.38 us
    all_to_all x2 -> x0, waiting for transfers between devices: 99.6 us -> none  [the longest x1 59.4 us: per_device(): lax.all_to_all(shares, SECTION, split_axis=0, concat_axis=0, tiled=True)]
    all_to_all x4 -> x6, blocking collectives: 106 us -> 199 us  [exchange(): return lax.all_to_all(value, axes, split_axis=0, concat_axis=0, tiled=True)]
    all_gather x1 -> x0, waiting for transfers between devices: 62.5 us -> none  [per_device(): weights = lax.all_gather(own, SECTION, axis=0, tiled=False)]
    all_to_all x2 -> x0, starting transfers between devices: 10.2 us -> none  [the longest x1 6.27 us: per_device(): lax.all_to_all(shares, SECTION, split_axis=0, concat_axis=0, tiled=True)]
    pallas_call x3 -> x5, Pallas kernels: 25.2 us -> 34.3 us  [the longest x1 25.2 us: chain(): pl.pallas_call(chain_kernel, out_shape=(side, side), in_specs=[SMEM, ANY,...]
    all_gather x1, waiting for transfers between devices: 0.01 us -> 7.29 us  [per_device(): gram = lax.all_gather(blocks, SECTION, axis=0, tiled=False)]
    ppermute x0 -> x2, waiting for transfers between devices: none -> 7 us  [the longest x1 4.11 us: per_device(): received = lax.ppermute(other, 'c', cores)]
    unnamed x24 -> x26, local copies, waits for them, and re-layouts: 7.15 us -> 3.88 us
  transfers between devices with their start and end apart: 4 -> 3, of which waited for: 3 -> 3; matrix products, arithmetic and copies ran while one was open for 1% -> 1% of each run, Pallas kernels for 1% -> 2%
where the time goes in v2:
time: 273 us; the launch traced here: 271 us
  blocking collectives  199 us (73%)
  Pallas kernels  34.3 us (13%)
  waiting for transfers between devices  14.3 us (5%)
  between operations  14.2 us (5%)
  local copies, waits for them, and re-layouts  5.46 us (2%)
  other arithmetic  3.38 us (1%)
    all_to_all x6, blocking collectives, exchange(): return lax.all_to_all(value, axes, split_axis=0, concat_axis=0, tiled=True)  199 us
    pallas_call x1, Pallas kernels, chain(): pl.pallas_call(chain_kernel, out_shape=(side, side), in_specs=[SMEM, ANY,...  25.2 us
    all_gather x1, waiting for transfers between devices, per_device(): gram = lax.all_gather(blocks, SECTION, axis=0, tiled=False)  7.29 us
  transfers between devices with their start and end apart: 3, of which 3 were waited for; matrix products, arithmetic and copies ran while one was open for 1% of the time, Pallas kernels for 2%

profile of v2, /device:TPU:8, one launch (start us, length us, event | category | flops | bytes accessed | tf_op | source)
XLA Modules:
  0.0 270.8 jit_solution(10878401539023804681)
XLA Ops:
  7.2 0.0 all-gather.3.cloned.1.call-start
  7.2 0.7 dynamic-slice_convert_fusion.gain_ref
  7.9 0.9 copy-done.1
  8.9 0.9 copy-done.3
  9.8 0.2 weights.1
  10.0 33.7 %all_to_all.30.near_ref = bf16[8,256,512]{2,1,0:T(8,128)(2,1)S(1)} all-to-all(bf16[8,256,512]{2,1,0:T(8,128)(2,1)S(1)} %weights.1), channel_id=1, replica_groups=mesh['xh'=2,'y'=4,'c'=2,'xl'=2,'z'=8] {'xh','y'}, dimensions={0} | all-to-all | bytes 4194304 | tf_op jit(solution)/shard_map/weights/all_to_all | solution.py:407
  43.7 0.1 pad_add_fusion.index_ref
  43.8 1.3 constant_dynamic-slice_fusion
  45.1 2.9 %collective-permute-done.far_ref = bf16[8,256,512]{2,1,0:T(8,128)(2,1)} collective-permute-done((bf16[8,256,512]{2,1,0:T(8,128)(2,1)S(1)}, bf16[8,256,512]{2,1,0:T(8,128)(2,1)}, u32[]{:S(2)}, u32[]{:S(2)}) %collective-permute-start) | collective-permute-done | bytes 2097184 | tf_op jit(solution)/shard_map/weights/ppermute | solution.py:414
  48.0 3.1 %gram.1 = bf16[16,208,128]{2,1,0:T(8,128)(2,1)S(1)} custom-call(s32[2]{0:T(128)S(1)} %pad_add_fusion.index_ref, bf16[8,256,512]{2,1,0:T(8,128)(2,1)S(1)} %all_to_all.30.near_ref, bf16[8,256,512]{2,1,0:T(8,128)(2,1)} %collective-permute-done.far_ref, bf16[16,8192]{1,0:T(8,128)(2,1)S(1)} %pad_maximum_fusion.both_ref), custom_call_target="tpu_custom_call" | custom-call | flops 268435456 | bytes 6291456 | tf_op jit(solution)/shard_map/gram/pallas_call | solution.py:131
  51.1 31.6 %all_to_all.31.packed_ref = bf16[16,208,128]{2,1,0:T(8,128)(2,1)S(1)} all-to-all(bf16[16,208,128]{2,1,0:T(8,128)(2,1)S(1)} %gram.1), channel_id=1, replica_groups=mesh['xh'=2,'y'=4,'c'=2,'xl'=2,'z'=8] {'xl','z'}, dimensions={0} | all-to-all | bytes 1703936 | tf_op jit(solution)/shard_map/gram/all_to_all | solution.py:407
  82.7 0.1 slice_reduce_fusion
  82.8 0.1 broadcast_in_dim.4
  82.9 20.0 %all_to_all.32 = bf16[16,128,128]{2,1,0:T(8,128)(2,1)} all-to-all(bf16[16,128,128]{2,1,0:T(8,128)(2,1)S(1)} %broadcast_in_dim.4), channel_id=1, replica_groups=mesh['xh'=2,'y'=4,'c'=2,'xl'=2,'z'=8] {'xl','z'}, dimensions={0} | all-to-all | bytes 1048576 | tf_op jit(solution)/shard_map/gram/all_to_all | solution.py:407
  102.8 0.0 all-gather.3.cloned.1.call-update
  102.9 4.2 %project.1 = (bf16[16,128,384]{2,1,0:T(8,128)(2,1)S(1)}, bf16[128,512]{1,0:T(8,128)(2,1)S(1)}, bf16[128,512]{1,0:T(8,128)(2,1)S(1)}, f32[128,128]{1,0:T(8,128)S(1)}) custom-call(s32[2]{0:T(128)S(1)} %pad_add_fusion.index_ref, bf16[16,208,128]{2,1,0:T(8,128)(2,1)S(1)} %all_to_all.31.packed_ref, bf16[8,256,512]{2,1,0:T(8,128)(2,1)S(1)} %all_to_all.30.near_ref, ...), custom_call_target="tpu_custom_call" | custom-call | flops 805306368 | bytes 7340032 | tf_op jit(solution)/shard_map/project/pallas_call | solution.py:180
  107.2 0.6 copy-done.10
  107.8 0.7 copy-done.11
  108.5 0.6 copy-done.12
  109.1 41.1 %all_to_all.33 = bf16[16,128,384]{2,1,0:T(8,128)(2,1)S(1)} all-to-all(bf16[16,128,384]{2,1,0:T(8,128)(2,1)S(1)} %get-tuple-element.12), channel_id=1, replica_groups=mesh['xh'=2,'y'=4,'c'=2,'xl'=2,'z'=8] {'xl','z'}, dimensions={0} | all-to-all | bytes 3145728 | tf_op jit(solution)/shard_map/project/all_to_all | solution.py:407
  150.2 0.2 reduce_sum.25
  150.4 0.2 broadcast_in_dim.5
  150.6 41.4 %all_to_all.34.proj_ref = bf16[16,128,384]{2,1,0:T(8,128)(2,1)} all-to-all(bf16[16,128,384]{2,1,0:T(8,128)(2,1)S(1)} %broadcast_in_dim.5), channel_id=1, replica_groups=mesh['xh'=2,'y'=4,'c'=2,'xl'=2,'z'=8] {'xl','z'}, dimensions={0} | all-to-all | bytes 3145728 | tf_op jit(solution)/shard_map/project/all_to_all | solution.py:407
  192.0 7.3 %all-gather.3.cloned.1.call-done = bf16[256,128,128]{2,1,0:T(8,128)(2,1)} async-done(((bf16[16,128,128]{2,1,0:T(8,128)(2,1)}), bf16[256,128,128]{2,1,0:T(8,128)(2,1)}) %all-gather.3.cloned.1.call-update) | async-done | bytes 8388624 | tf_op jit(solution)/shard_map/gram/all_gather | solution.py:427
  199.3 25.2 %chain.1 = (bf16[8,256,512]{2,1,0:T(8,128)(2,1)}, bf16[8,256,512]{2,1,0:T(8,128)(2,1)}) custom-call(s32[2]{0:T(128)} %copy-done.9, bf16[16,16,128,128]{3,2,1,0:T(8,128)(2,1)} %bitcast.7, bf16[16,128,384]{2,1,0:T(8,128)(2,1)} %all_to_all.34.proj_ref, f32[128,128]{1,0:T(8,128)} %copy-done.12, bf16[8,256,512]{2,1,0:T(8,128)(2,1)} %copy-done, ...), custom_call_target="tpu_custom_call" | custom-call | flops 4294967296 | bytes 20971520 | tf_op jit(solution)/shard_map/chain/pallas_call | solution.py:332
  224.5 0.3 collective-permute-start.1
  224.9 4.1 %collective-permute-done.1 = bf16[8,256,512]{2,1,0:T(8,128)(2,1)S(1)} collective-permute-done((bf16[8,256,512]{2,1,0:T(8,128)(2,1)}, bf16[8,256,512]{2,1,0:T(8,128)(2,1)S(1)}, u32[]{:S(2)}, u32[]{:S(2)}) %collective-permute-start.1) | collective-permute-done | bytes 2097184 | tf_op jit(solution)/shard_map/sum/ppermute | solution.py:437
  229.0 2.3 add_convert_fusion
  231.3 0.0 copy-start.4
  231.3 0.0 copy-start.5
  231.4 30.9 %all_to_all.35.parts_ref = bf16[8,256,512]{2,1,0:T(8,128)(2,1)S(1)} all-to-all(bf16[8,256,512]{2,1,0:T(8,128)(2,1)S(1)} %add_convert_fusion), channel_id=1, replica_groups=mesh['xh'=2,'y'=4,'c'=2,'xl'=2,'z'=8] {'xh','y'}, dimensions={0} | all-to-all | bytes 4194304 | tf_op jit(solution)/shard_map/sum/all_to_all | solution.py:407
  262.3 1.6 adam.1
  (21 shorter events, 0.1 us)
Async XLA Ops:
  7.2 192.2 %all-gather.3.cloned.1.call-start = ((), (), s32[]{:S(2)}) async-start(), calls=%async_computation.6 | async-start | bytes 8912896 | tf_op jit(solution)/shard_map/gram/all_gather | solution.py:427
  7.9 0.9 copy-start.1
  8.9 0.9 copy-start.3
  43.7 59.1 %copy-start = (bf16[8,256,512]{2,1,0:T(8,128)(2,1)}, bf16[8,256,512]{2,1,0:T(8,128)(2,1)S(1)}, u32[]{:S(2)}) copy-start(bf16[8,256,512]{2,1,0:T(8,128)(2,1)S(1)} %all_to_all.30.near_ref) | copy-start | bytes 6291460
  43.7 4.3 %collective-permute-start = (bf16[8,256,512]{2,1,0:T(8,128)(2,1)S(1)}, bf16[8,256,512]{2,1,0:T(8,128)(2,1)}, u32[]{:S(2)}, u32[]{:S(2)}) collective-permute-start(bf16[8,256,512]{2,1,0:T(8,128)(2,1)S(1)} %all_to_all.30.near_ref), channel_id=1, source_target_pairs={{0,16},{16,0},{1,17},{17,1},{2,18},{18,2},{3,19},{19,3},{4,20},{20... | collective-permute-start | bytes 6291464 | tf_op jit(solution)/shard_map/weights/ppermute | solution.py:414
  43.8 59.1 %copy-start.9 = (s32[2]{0:T(128)}, s32[2]{0:T(128)S(1)}, u32[]{:S(2)}) copy-start(s32[2]{0:T(128)S(1)} %pad_add_fusion.index_ref) | copy-start | bytes 28
  107.1 0.7 copy-start.10
  107.8 0.7 copy-start.11
  108.5 0.6 copy-start.12
  224.5 4.5 %collective-permute-start.1 = (bf16[8,256,512]{2,1,0:T(8,128)(2,1)}, bf16[8,256,512]{2,1,0:T(8,128)(2,1)S(1)}, u32[]{:S(2)}, u32[]{:S(2)}) collective-permute-start(bf16[8,256,512]{2,1,0:T(8,128)(2,1)} %get-tuple-element.17), channel_id=1, source_target_pairs={{0,16},{16,0},{1,17},{17,1},{2,18},{18,2},{3,19},{19,3},{4,20},{20... | collective-permute-start | bytes 6291464 | tf_op jit(solution)/shard_map/sum/ppermute | solution.py:437
  231.3 31.0 %copy-start.2 = (f32[1,512,128]{2,1,0:T(8,128)S(1)}, f32[1,512,128]{2,1,0:T(8,128)}, u32[]{:S(2)}) copy-start(f32[1,512,128]{2,1,0:T(8,128)} %refs_0_.1) | copy-start | bytes 786436
  231.3 31.0 %copy-start.4 = (f32[1,128,512]{2,1,0:T(8,128)S(1)}, f32[1,128,512]{2,1,0:T(8,128)}, u32[]{:S(2)}) copy-start(f32[1,128,512]{2,1,0:T(8,128)} %refs_3_.1) | copy-start | bytes 786436
  231.3 31.0 %copy-start.5 = (f32[1,512,128]{2,1,0:T(8,128)S(1)}, f32[1,512,128]{2,1,0:T(8,128)}, u32[]{:S(2)}) copy-start(f32[1,512,128]{2,1,0:T(8,128)} %refs_1_.1) | copy-start | bytes 786436
  231.3 30.9 %copy-start.6 = (f32[1,512,128]{2,1,0:T(8,128)S(1)}, f32[1,512,128]{2,1,0:T(8,128)}, u32[]{:S(2)}) copy-start(f32[1,512,128]{2,1,0:T(8,128)} %refs_2_.1) | copy-start | bytes 786436
  231.3 30.9 %copy-start.7 = (f32[1,128,512]{2,1,0:T(8,128)S(1)}, f32[1,128,512]{2,1,0:T(8,128)}, u32[]{:S(2)}) copy-start(f32[1,128,512]{2,1,0:T(8,128)} %refs_4_.1) | copy-start | bytes 786436
  231.4 30.9 %copy-start.8 = (f32[1,128,512]{2,1,0:T(8,128)S(1)}, f32[1,128,512]{2,1,0:T(8,128)}, u32[]{:S(2)}) copy-start(f32[1,128,512]{2,1,0:T(8,128)} %refs_5_.1) | copy-start | bytes 786436
Sparse Core Ops, SparseCore 0:
  103.0 96.2 all-gather.2

commit v3 on v2

--- a/solution.py
+++ b/solution.py
@@ -20,7 +20,11 @@
 CHUNK = 128
 OWN_ROWS = CHUNK // PARTS
 HALF = LAYERS // 2
-PACKED = RANK + 4 * 2 * OWN_ROWS + 2 * OWN_ROWS
+PIECE = HALF * RANK // PARTS
+LANES = 2 * RANK
+SPANS = SLICE // LANES
+TAIL = PIECE + SPANS * 2 * OWN_ROWS
+PACKED = TAIL + 2 * OWN_ROWS
 
 SECTION = ("xh", "y", "c")
 DP = ("xl", "z")
@@ -89,22 +93,22 @@
     copies = load_weights(index_ref[1], near_ref, far_ref, weights, sems)
     both = both_ref[...]
     for part in range(PARTS):
-        for lane in range(SLICE // 128):
-            first = RANK + 2 * OWN_ROWS * lane
-            start = SLICE * part + 128 * lane
-            out_ref[part, first : first + 2 * OWN_ROWS, :] = both[:, start : start + 128]
+        for span in range(SPANS):
+            first = PIECE + 2 * OWN_ROWS * span
+            start = SLICE * part + LANES * span
+            out_ref[part, first : first + 2 * OWN_ROWS, :] = both[:, start : start + LANES]
     wide = both.astype(F32)[:OWN_ROWS]
     square = jnp.sum(wide * wide, axis=1, keepdims=True)
     high = square.astype(BF).astype(F32)
     tail = jnp.concatenate(
         [
-            jnp.broadcast_to(high, (OWN_ROWS, RANK)),
-            jnp.broadcast_to(square - high, (OWN_ROWS, RANK)),
+            jnp.broadcast_to(high, (OWN_ROWS, LANES)),
+            jnp.broadcast_to(square - high, (OWN_ROWS, LANES)),
         ],
         axis=0,
     ).astype(BF)
     for part in range(PARTS):
-        out_ref[part, PACKED - 2 * OWN_ROWS :, :] = tail
+        out_ref[part, TAIL:, :] = tail
     for copy in copies:
         copy.wait()
 
@@ -112,25 +116,26 @@
         return weights[lax.rem(layer, 2), layer // 2, rows, :]
 
     leave = pl.ds(RANK, RANK)
-    out_ref[0, :RANK, :] = nt(layer_rows(section, leave), layer_rows(section, leave)).astype(BF)
-    for reach in range(1, HALF + 1):
+    for reach in range(HALF):
         other = lax.rem(section + reach, LAYERS)
-        low = jnp.minimum(section, other)
-        high = jnp.maximum(section, other)
-        if reach < HALF:
-            block = nt(layer_rows(low, leave), layer_rows(high, pl.ds(0, 2 * RANK))).astype(BF)
-            out_ref[2 * reach - 1, :RANK, :] = block[:, :RANK]
-            out_ref[2 * reach, :RANK, :] = block[:, RANK:]
+        low = layer_rows(jnp.minimum(section, other), leave)
+        if reach > 0:
+            block = nt(low, layer_rows(jnp.maximum(section, other), pl.ds(0, 2 * RANK)))
         else:
+            across = lax.rem(section + HALF, LAYERS)
             start = pl.multiple_of((section // HALF) * RANK, RANK)
-            block = nt(layer_rows(low, leave), layer_rows(high, pl.ds(start, RANK)))
-            out_ref[2 * reach - 1, :RANK, :] = block.astype(BF)
+            far_rows = layer_rows(jnp.maximum(section, across), pl.ds(start, RANK))
+            near_rows = layer_rows(jnp.minimum(section, across), leave)
+            block = jnp.concatenate([nt(near_rows, far_rows), nt(low, low)], axis=1)
+        block = block.astype(BF)
+        out_ref[2 * reach, :PIECE, :] = block[:PIECE]
+        out_ref[2 * reach + 1, :PIECE, :] = block[PIECE:]
 
 
 def gram_and_rows(index, near, far, both):
     return pl.pallas_call(
         gram_kernel,
-        out_shape=jax.ShapeDtypeStruct((PARTS, PACKED, RANK), BF),
+        out_shape=jax.ShapeDtypeStruct((PARTS, PACKED, LANES), BF),
         in_specs=[SMEM, ANY, ANY, VMEM],
         out_specs=VMEM,
         scratch_shapes=[
@@ -142,31 +147,20 @@
     )(index, near, far, both)
 
 
-def block_place(low, high, half):
-    reach = high - low
-    if reach == 0:
-        return (low, 0)
-    if reach < HALF:
-        return (low, 2 * reach - 1 + half)
-    if reach == HALF:
-        return ((low, high)[half], LAYERS - 1)
-    return (high, 2 * (LAYERS - reach) - 1 + half)
-
-
 def project_kernel(
     index_ref, packed_ref, near_ref, far_ref, out_ref, rows_ref, grads_ref, square_ref, weights, sems
 ):
     copies = load_weights(index_ref[1], near_ref, far_ref, weights, sems)
     lanes = []
-    for lane in range(SLICE // 128):
-        first = RANK + 2 * OWN_ROWS * lane
+    for span in range(SPANS):
+        first = PIECE + 2 * OWN_ROWS * span
         lanes.append(packed_ref[:, first : first + 2 * OWN_ROWS, :].astype(F32))
     both = jnp.concatenate(lanes, axis=2)
     rows = both[:, :OWN_ROWS, :].reshape(CHUNK, SLICE).astype(BF)
     grads = both[:, OWN_ROWS:, :].reshape(CHUNK, SLICE).astype(BF)
     rows_ref[...] = rows
     grads_ref[...] = grads
-    tail = packed_ref[:, PACKED - 2 * OWN_ROWS :, :].astype(F32)
+    tail = packed_ref[:, TAIL:, :RANK].astype(F32)
     square_ref[...] = (tail[:, :OWN_ROWS, :] + tail[:, OWN_ROWS:, :]).reshape(CHUNK, RANK)
     for copy in copies:
         copy.wait()
@@ -198,53 +192,63 @@
 
 def chain_kernel(
     index_ref,
-    gram_hbm,
-    proj_ref,
-    square_ref,
-    near_ref,
-    far_ref,
-    rows_ref,
-    grads_ref,
-    keep_ref,
-    pass_ref,
-    gram,
-    weights,
-    shares,
-    hidden,
-    back,
-    pre_saved,
-    leave_saved,
-    rows_saved,
-    inv_saved,
-    gram_sems,
-    sems,
-    out_sems,
+    *refs,
 ):
+    block_refs = refs[:LAYERS]
+    (
+        proj_ref,
+        square_ref,
+        near_ref,
+        far_ref,
+        rows_ref,
+        grads_ref,
+        keep_ref,
+        pass_ref,
+        gram,
+        weights,
+        shares,
+        hidden,
+        back,
+        pre_saved,
+        leave_saved,
+        rows_saved,
+        inv_saved,
+        gram_sems,
+        sems,
+        out_sems,
+    ) = refs[LAYERS:]
     core = index_ref[1]
     copies = load_weights(core, near_ref, far_ref, weights, sems)
 
-    def fetch(layer):
-        for low in range(layer + 1):
-            for half in range(2):
-                if low == layer and half == 0:
-                    continue
-                place, slot = block_place(low, layer, half)
-                pltpu.make_async_copy(
-                    gram_hbm.at[place, slot],
-                    gram.at[
-                        pl.ds(low * RANK, RANK), pl.ds((2 * layer + half) * RANK, RANK)
-                    ],
-                    gram_sems.at[layer],
-                ).start()
+    plane, ring = index_ref[2], index_ref[3]
+
+    def place(ref, low, high, lane, width):
+        rows = pl.ds(pl.multiple_of(low * RANK, RANK), RANK)
+        first = pl.multiple_of((2 * high + lane) * RANK, RANK)
+        pltpu.make_async_copy(
+            ref, gram.at[rows, pl.ds(first, width)], gram_sems.at[high]
+        ).start()
+
+    def fetch(block_ref, step_plane, step_ring, step_core):
+        across_plane = plane if step_plane == 0 else 1 - plane
+        across_core = core if step_core == 0 else 1 - core
+        layer = (across_plane * 4 + lax.rem(ring + step_ring, 4)) * 2 + across_core
+        place(block_ref.at[0, :, pl.ds(RANK, RANK)], layer, layer, 1, RANK)
+        for reach in range(1, HALF):
+            other = lax.rem(layer + reach, LAYERS)
+            low, high = jnp.minimum(layer, other), jnp.maximum(layer, other)
+            place(block_ref.at[reach], low, high, 0, 2 * RANK)
+        other = lax.rem(layer + HALF, LAYERS)
+        low, high = jnp.minimum(layer, other), jnp.maximum(layer, other)
+        place(block_ref.at[0, :, pl.ds(0, RANK)], low, high, layer // HALF, RANK)
+
+    steps = [(core, plane, ring) for core in (0, 1) for plane in (0, 1) for ring in range(4)]
+    for (step_core, step_plane, step_ring), block_ref in zip(steps, block_refs):
+        fetch(block_ref, step_plane, step_ring, step_core)
 
     def arrived(layer):
         view = gram.at[pl.ds(0, (2 * layer + 1) * (RANK // 2)), pl.ds(0, 2 * RANK)]
         pltpu.make_async_copy(view, view, gram_sems.at[layer]).wait()
-
-    for layer in range(LAYERS):
-        fetch(layer)
-    for copy in copies:
-        copy.wait()
 
     square = square_ref[...][:, :1]
     wide = rows_ref[...].astype(F32)
@@ -275,6 +279,9 @@
             0.0,
         )
         rows_saved[layer] = wide.astype(BF)
+        if layer == 0:
+            for copy in copies:
+                copy.wait()
         if layer < LAYERS - 1:
             wide = wide + nn(act, weights[layer % 2, layer // 2, RANK:, :])
 
@@ -332,7 +339,7 @@
     return pl.pallas_call(
         chain_kernel,
         out_shape=(side, side),
-        in_specs=[SMEM, ANY, VMEM, VMEM, ANY, ANY, VMEM, VMEM],
+        in_specs=[SMEM] + [ANY] * LAYERS + [VMEM, VMEM, ANY, ANY, VMEM, VMEM],
         out_specs=(ANY, ANY),
         scratch_shapes=[
             pltpu.VMEM((LAYERS * RANK, 2 * LAYERS * RANK), BF),
@@ -350,7 +357,7 @@
         ],
         compiler_params=params(56),
         cost_estimate=cost(4 * 2**30, 20 * 2**20),
-    )(index, gram, proj, square, near, far, rows, grads)
+    )(index, *gram, proj, square, near, far, rows, grads)
 
 
 def adam_update(weight, moment, second, grad):
@@ -399,9 +406,11 @@
     section = lax.axis_index(SECTION)
     part = lax.axis_index(DP)
     core = lax.axis_index("c")
-    index = jnp.stack([section, core])
+    index = jnp.stack([section, core, lax.axis_index("xh"), lax.axis_index("y")])
     gain = lax.dynamic_slice_in_dim(norm_gain, part * SLICE, SLICE, axis=1).astype(F32)
-    cores = [(0, 1), (1, 0)]
+    swap = [(0, 1), (1, 0)]
+    up = [(i, (i + 1) % 4) for i in range(4)]
+    down = [(i, (i + 3) % 4) for i in range(4)]
 
     def exchange(value, axes):
         return lax.all_to_all(value, axes, split_axis=0, concat_axis=0, tiled=True)
@@ -411,7 +420,7 @@
 
     with jax.named_scope("weights"):
         near = exchange(own_weights(enter_weight, leave_weight, gain), ("xh", "y"))
-        far = lax.ppermute(near, "c", cores)
+        far = lax.ppermute(near, "c", swap)
 
     with jax.named_scope("gram"):
         both = jnp.concatenate(
@@ -423,18 +432,30 @@
             ]
         )
         packed = exchange(gram_and_rows(index, near, far, both), DP)
-        blocks = spread(jnp.sum(packed[:, :RANK, :].astype(F32), axis=0).astype(BF))
-        gram = lax.all_gather(blocks, SECTION, axis=0, tiled=False)
+        blocks = spread(jnp.sum(packed[:, :PIECE, :].astype(F32), axis=0).astype(BF))
+        blocks = blocks.reshape(HALF, RANK, LANES)
+        other = lax.ppermute(blocks, "xh", swap)
 
     with jax.named_scope("project"):
         proj, rows, grads, square = project(index, packed, near, far)
-        proj = spread(jnp.sum(exchange(proj, DP).astype(F32), axis=0).astype(BF))
+
+        def ring(value):
+            below = lax.ppermute(value, "y", up)
+            above = lax.ppermute(value, "y", down)
+            return [value, above, lax.ppermute(above, "y", down), below]
+
+        plane = ring(blocks)
+        other, _ = lax.optimization_barrier((other, proj))
+        gram = plane + ring(other)
+        gram = gram + [lax.ppermute(value, "c", swap) for value in gram]
+        proj, _, _ = lax.optimization_barrier((exchange(proj, DP), other, plane[2]))
+        proj = spread(jnp.sum(proj.astype(F32), axis=0).astype(BF))
 
     with jax.named_scope("chain"):
         keep, other = chain(index, gram, proj, square, near, far, rows, grads)
 
     with jax.named_scope("sum"):
-        received = lax.ppermute(other, "c", cores)
+        received = lax.ppermute(other, "c", swap)
         parts = exchange((keep.astype(F32) + received.astype(F32)).astype(BF), ("xh", "y"))
 
     with jax.named_scope("adam"):

time: 273 us -> 254 us (0.930)
  blocking collectives: 199 us -> 98.6 us
  waiting for transfers between devices: 14.3 us -> 77.8 us
  starting transfers between devices: 0.38 us -> 25.9 us
  between operations: 14.2 us -> 0.96 us
  local copies, waits for them, and re-layouts: 5.46 us -> 11.4 us
    all_to_all x6 -> x3, blocking collectives: 199 us -> 98.6 us  [exchange(): return lax.all_to_all(value, axes, split_axis=0, concat_axis=0, tiled=True)]
    ppermute x2 -> x17, waiting for transfers between devices: 7 us -> 52.3 us  [the longest x2 22.9 us: ring(): below = lax.ppermute(value, 'y', up)]
    all_to_all x0 -> x3, waiting for transfers between devices: none -> 25.5 us  [exchange(): return lax.all_to_all(value, axes, split_axis=0, concat_axis=0, tiled=True)]
    all_to_all x0 -> x3, starting transfers between devices: none -> 14.3 us  [exchange(): return lax.all_to_all(value, axes, split_axis=0, concat_axis=0, tiled=True)]
    ppermute x2 -> x17, starting transfers between devices: 0.35 us -> 11.7 us  [the longest x2 4.29 us: ring(): return [value, above, lax.ppermute(above, 'y', down), below]]
    all_gather x1 -> x0, waiting for transfers between devices: 7.29 us -> none  [per_device(): gram = lax.all_gather(blocks, SECTION, axis=0, tiled=False)]
    unnamed x26 -> x60, local copies, waits for them, and re-layouts: 3.88 us -> 7.8 us
  transfers between devices with their start and end apart: 3 -> 20, of which waited for: 3 -> 11; matrix products, arithmetic and copies ran while one was open for 1% -> 1% of each run, Pallas kernels for 2% -> 2%
where the time goes in v3:
time: 254 us; the launch traced here: 253 us
  blocking collectives  98.6 us (39%)
  waiting for transfers between devices  77.8 us (31%)
  Pallas kernels  34.6 us (14%)
  starting transfers between devices  25.9 us (10%)
  local copies, waits for them, and re-layouts  11.4 us (4%)
  other arithmetic  3.38 us (1%)
    all_to_all x3, blocking collectives, exchange(): return lax.all_to_all(value, axes, split_axis=0, concat_axis=0, tiled=True)  98.6 us
    all_to_all x3, waiting for transfers between devices, exchange(): return lax.all_to_all(value, axes, split_axis=0, concat_axis=0, tiled=True)  25.5 us
    pallas_call x1, Pallas kernels, chain(): pl.pallas_call(chain_kernel, out_shape=(side, side), in_specs=[SMEM] + [A...  25.4 us
    ppermute x2, waiting for transfers between devices, ring(): below = lax.ppermute(value, 'y', up)  22.9 us
    all_to_all x3, starting transfers between devices, exchange(): return lax.all_to_all(value, axes, split_axis=0, concat_axis=0, tiled=True)  14.3 us
    ppermute x1, waiting for transfers between devices, per_device(): other = lax.ppermute(blocks, 'xh', swap)  10.5 us
    ppermute x2, waiting for transfers between devices, ring(): above = lax.ppermute(value, 'y', down)  10.2 us
    unnamed x60, local copies, waits for them, and re-layouts  7.8 us
  transfers between devices with their start and end apart: 20, of which 11 were waited for; matrix products, arithmetic and copies ran while one was open for 1% of the time, Pallas kernels for 2%

profile of v3, /device:TPU:8, one launch (start us, length us, event | category | flops | bytes accessed | tf_op | source)
XLA Modules:
  0.0 252.6 jit_solution(3829278792107846718)
XLA Ops:
  1.3 0.9 copy-done.2
  2.3 0.9 copy-done.4
  3.4 33.7 %all_to_all.30.near_ref.refs_18_ = bf16[8,256,512]{2,1,0:T(8,128)(2,1)S(1)} all-to-all(bf16[8,256,512]{2,1,0:T(8,128)(2,1)S(1)} %weights.1), channel_id=1, replica_groups=mesh['xh'=2,'y'=4,'c'=2,'xl'=2,'z'=8] {'xh','y'}, dimensions={0} | all-to-all | bytes 4194304 | tf_op jit(solution)/shard_map/weights/all_to_all | solution.py:416
  37.2 1.3 constant_dynamic-slice_fusion
  38.6 2.9 %collective-permute-done.far_ref.refs_19_ = bf16[8,256,512]{2,1,0:T(8,128)(2,1)} collective-permute-done((bf16[8,256,512]{2,1,0:T(8,128)(2,1)S(1)}, bf16[8,256,512]{2,1,0:T(8,128)(2,1)}, u32[]{:S(2)}, u32[]{:S(2)}) %collective-permute-start) | collective-permute-done | bytes 2097184 | tf_op jit(solution)/shard_map/weights/ppermute | solution.py:423
  41.4 3.1 %gram.1 = bf16[16,112,256]{2,1,0:T(8,128)(2,1)S(1)} custom-call(s32[4]{0:T(128)S(1)} %pad_add_fusion.index_ref, bf16[8,256,512]{2,1,0:T(8,128)(2,1)S(1)} %all_to_all.30.near_ref.refs_18_, bf16[8,256,512]{2,1,0:T(8,128)(2,1)} %collective-permute-done.far_ref.refs_19_, bf16[16,8192]{1,0:T(8,128)(2,1)S(1)} %pad_maximum_fusion.both_ref), custom_call_target="tpu_custom_call" | custom-call | flops 268435456 | bytes 6291456 | tf_op jit(solution)/shard_map/gram/pallas_call | solution.py:136
  44.5 33.1 %all_to_all.31.packed_ref = bf16[16,112,256]{2,1,0:T(8,128)(2,1)S(1)} all-to-all(bf16[16,112,256]{2,1,0:T(8,128)(2,1)S(1)} %gram.1), channel_id=1, replica_groups=mesh['xh'=2,'y'=4,'c'=2,'xl'=2,'z'=8] {'xl','z'}, dimensions={0} | all-to-all | bytes 1835008 | tf_op jit(solution)/shard_map/gram/all_to_all | solution.py:416
  78.6 4.5 %all-to-all-start.2 = ((bf16[16,64,256]{2,1,0:T(8,128)(2,1)}), bf16[16,64,256]{2,1,0:T(8,128)(2,1)S(1)}, u32[]{:S(2)}, u32[]{:S(2)}) async-start(bf16[16,64,256]{2,1,0:T(8,128)(2,1)} %broadcast_in_dim.4), calls=%async_computation.2 | async-start | bytes 1048576 | tf_op jit(solution)/shard_map/gram/all_to_all | solution.py:416
  83.1 4.2 %project.1 = (bf16[16,128,384]{2,1,0:T(8,128)(2,1)S(1)}, bf16[128,512]{1,0:T(8,128)(2,1)S(1)}, bf16[128,512]{1,0:T(8,128)(2,1)S(1)}, f32[128,128]{1,0:T(8,128)S(1)}) custom-call(s32[4]{0:T(128)S(1)} %pad_add_fusion.index_ref, bf16[16,112,256]{2,1,0:T(8,128)(2,1)S(1)} %all_to_all.31.packed_ref, bf16[8,256,512]{2,1,0:T(8,128)(2,1)S(1)} %all_to_all.30.near_ref.refs_18_, ...), custom_call_target="tpu_custom_call" | custom-call | flops 805306368 | bytes 7340032 | tf_op jit(solution)/shard_map/project/pallas_call | solution.py:174
  87.4 1.2 copy-done.1
  90.5 8.2 %all-to-all-done.2 = bf16[16,64,256]{2,1,0:T(8,128)(2,1)S(1)} async-done(((bf16[16,64,256]{2,1,0:T(8,128)(2,1)}), bf16[16,64,256]{2,1,0:T(8,128)(2,1)S(1)}, u32[]{:S(2)}, u32[]{:S(2)}) %all-to-all-start.2) | async-done | bytes 524320 | tf_op jit(solution)/shard_map/gram/all_to_all | solution.py:416
  98.8 4.7 %all-to-all-start.3 = ((bf16[16,128,384]{2,1,0:T(8,128)(2,1)}), bf16[16,128,384]{2,1,0:T(8,128)(2,1)S(1)}, u32[]{:S(2)}, u32[]{:S(2)}) async-start(bf16[16,128,384]{2,1,0:T(8,128)(2,1)} %copy-done.1), calls=%async_computation.3 | async-start | bytes 3145728 | tf_op jit(solution)/shard_map/project/all_to_all | solution.py:416
  103.4 1.9 collective-permute-start.1
  105.3 1.0 collective-permute-start.4
  106.3 10.2 %collective-permute-done.1.refs_1_ = bf16[8,128,256]{2,1,0:T(8,128)(2,1)S(1)} collective-permute-done((bf16[8,128,256]{2,1,0:T(8,128)(2,1)S(1)}, bf16[8,128,256]{2,1,0:T(8,128)(2,1)S(1)}, u32[]{:S(2)}, u32[]{:S(2)}) %collective-permute-start.1) | collective-permute-done | bytes 524320 | tf_op jit(solution)/shard_map/project/ppermute | solution.py:444
  116.5 1.8 collective-permute-start.2
  118.3 10.5 %collective-permute-done.4.refs_4_ = bf16[8,128,256]{2,1,0:T(8,128)(2,1)S(1)} collective-permute-done((bf16[8,128,256]{2,1,0:T(8,128)(2,1)S(1)}, bf16[8,128,256]{2,1,0:T(8,128)(2,1)S(1)}, u32[]{:S(2)}, u32[]{:S(2)}) %collective-permute-start.4) | collective-permute-done | bytes 524320 | tf_op jit(solution)/shard_map/gram/ppermute | solution.py:437
  129.6 11.2 %all-to-all-done.3 = bf16[16,128,384]{2,1,0:T(8,128)(2,1)S(1)} async-done(((bf16[16,128,384]{2,1,0:T(8,128)(2,1)}), bf16[16,128,384]{2,1,0:T(8,128)(2,1)S(1)}, u32[]{:S(2)}, u32[]{:S(2)}) %all-to-all-start.3) | async-done | bytes 1572896 | tf_op jit(solution)/shard_map/project/all_to_all | solution.py:416
  141.0 1.4 broadcast_in_dim.5
  142.4 5.1 %all-to-all-start.4 = ((bf16[16,128,384]{2,1,0:T(8,128)(2,1)}), bf16[16,128,384]{2,1,0:T(8,128)(2,1)S(1)}, u32[]{:S(2)}, u32[]{:S(2)}) async-start(bf16[16,128,384]{2,1,0:T(8,128)(2,1)} %broadcast_in_dim.5), calls=%async_computation.4 | async-start | bytes 3145728 | tf_op jit(solution)/shard_map/project/all_to_all | solution.py:416
  148.2 1.4 collective-permute-start.5
  149.6 11.6 %collective-permute-done.3.refs_3_ = bf16[8,128,256]{2,1,0:T(8,128)(2,1)S(1)} collective-permute-done((bf16[8,128,256]{2,1,0:T(8,128)(2,1)S(1)}, bf16[8,128,256]{2,1,0:T(8,128)(2,1)S(1)}, u32[]{:S(2)}, u32[]{:S(2)}) %collective-permute-start.3) | collective-permute-done | bytes 524320 | tf_op jit(solution)/shard_map/project/ppermute | solution.py:443
  162.3 2.5 collective-permute-start.6
  165.6 11.3 %collective-permute-done.7.refs_7_ = bf16[8,128,256]{2,1,0:T(8,128)(2,1)S(1)} collective-permute-done((bf16[8,128,256]{2,1,0:T(8,128)(2,1)S(1)}, bf16[8,128,256]{2,1,0:T(8,128)(2,1)S(1)}, u32[]{:S(2)}, u32[]{:S(2)}) %collective-permute-start.7) | collective-permute-done | bytes 524320 | tf_op jit(solution)/shard_map/project/ppermute | solution.py:443
  177.4 1.4 collective-permute-done.15.refs_15_
  179.7 6.1 %all-to-all-done.4.refs_16_ = bf16[16,128,384]{2,1,0:T(8,128)(2,1)S(1)} async-done(((bf16[16,128,384]{2,1,0:T(8,128)(2,1)}), bf16[16,128,384]{2,1,0:T(8,128)(2,1)S(1)}, u32[]{:S(2)}, u32[]{:S(2)}) %all-to-all-start.4) | async-done | bytes 1572896 | tf_op jit(solution)/shard_map/project/all_to_all | solution.py:416
  185.8 1.1 copy-done.14
  186.9 25.4 %chain.1 = (bf16[8,256,512]{2,1,0:T(8,128)(2,1)}, bf16[8,256,512]{2,1,0:T(8,128)(2,1)}) custom-call(s32[4]{0:T(128)} %copy-done.10, bf16[8,128,256]{2,1,0:T(8,128)(2,1)} %bitcast.11, bf16[8,128,256]{2,1,0:T(8,128)(2,1)} %copy-done.16, bf16[8,128,256]{2,1,0:T(8,128)(2,1)} %collective-permute-done.2.refs_2_, bf16[8,128,256]{2,1,0:T(8,128)(2,1)} %copy-done.19, ...), custom_call_target="tpu_custom_call" | custom-call | flops 4294967296 | bytes 20971520 | tf_op jit(solution)/shard_map/chain/pallas_call | solution.py:339
  212.5 4.4 %collective-permute-done.16 = bf16[8,256,512]{2,1,0:T(8,128)(2,1)S(1)} collective-permute-done((bf16[8,256,512]{2,1,0:T(8,128)(2,1)}, bf16[8,256,512]{2,1,0:T(8,128)(2,1)S(1)}, u32[]{:S(2)}, u32[]{:S(2)}) %collective-permute-start.16) | collective-permute-done | bytes 2097184 | tf_op jit(solution)/shard_map/sum/ppermute | solution.py:458
  216.8 2.3 add_convert_fusion
  219.2 31.7 %all_to_all.32.parts_ref = bf16[8,256,512]{2,1,0:T(8,128)(2,1)S(1)} all-to-all(bf16[8,256,512]{2,1,0:T(8,128)(2,1)S(1)} %add_convert_fusion), channel_id=1, replica_groups=mesh['xh'=2,'y'=4,'c'=2,'xl'=2,'z'=8] {'xh','y'}, dimensions={0} | all-to-all | bytes 4194304 | tf_op jit(solution)/shard_map/sum/all_to_all | solution.py:416
  251.0 1.6 adam.1
  (85 shorter events, 8.9 us)
Async XLA Ops:
  37.1 46.0 %copy-start = (bf16[8,256,512]{2,1,0:T(8,128)(2,1)}, bf16[8,256,512]{2,1,0:T(8,128)(2,1)S(1)}, u32[]{:S(2)}) copy-start(bf16[8,256,512]{2,1,0:T(8,128)(2,1)S(1)} %all_to_all.30.near_ref.refs_18_) | copy-start | bytes 6291460
  37.1 4.3 %collective-permute-start = (bf16[8,256,512]{2,1,0:T(8,128)(2,1)S(1)}, bf16[8,256,512]{2,1,0:T(8,128)(2,1)}, u32[]{:S(2)}, u32[]{:S(2)}) collective-permute-start(bf16[8,256,512]{2,1,0:T(8,128)(2,1)S(1)} %all_to_all.30.near_ref.refs_18_), channel_id=1, source_target_pairs={{0,16},{16,0},{1,17},{17,1},{2,18},{18,2},{3,19},{19,3},{4,20},{20... | collective-permute-start | bytes 6291464 | tf_op jit(solution)/shard_map/weights/ppermute | solution.py:423
  37.2 45.9 %copy-start.10 = (s32[4]{0:T(128)}, s32[4]{0:T(128)S(1)}, u32[]{:S(2)}) copy-start(s32[4]{0:T(128)S(1)} %pad_add_fusion.index_ref) | copy-start | bytes 52
  78.6 20.2 %all-to-all-start.2 = ((bf16[16,64,256]{2,1,0:T(8,128)(2,1)}), bf16[16,64,256]{2,1,0:T(8,128)(2,1)S(1)}, u32[]{:S(2)}, u32[]{:S(2)}) async-start(bf16[16,64,256]{2,1,0:T(8,128)(2,1)} %broadcast_in_dim.4), calls=%async_computation.2 | async-start | bytes 1048576 | tf_op jit(solution)/shard_map/gram/all_to_all | solution.py:416
  98.8 50.9 %copy-start.15 = (bf16[16,64,256]{2,1,0:T(8,128)(2,1)}, bf16[16,64,256]{2,1,0:T(8,128)(2,1)S(1)}, u32[]{:S(2)}) copy-start(bf16[16,64,256]{2,1,0:T(8,128)(2,1)S(1)} %all-to-all-done.2) | copy-start | bytes 1572868
  98.8 42.0 %all-to-all-start.3 = ((bf16[16,128,384]{2,1,0:T(8,128)(2,1)}), bf16[16,128,384]{2,1,0:T(8,128)(2,1)S(1)}, u32[]{:S(2)}, u32[]{:S(2)}) async-start(bf16[16,128,384]{2,1,0:T(8,128)(2,1)} %copy-done.1), calls=%async_computation.3 | async-start | bytes 3145728 | tf_op jit(solution)/shard_map/project/all_to_all | solution.py:416
  103.4 13.0 %collective-permute-start.1 = (bf16[8,128,256]{2,1,0:T(8,128)(2,1)S(1)}, bf16[8,128,256]{2,1,0:T(8,128)(2,1)S(1)}, u32[]{:S(2)}, u32[]{:S(2)}) collective-permute-start(bf16[8,128,256]{2,1,0:T(8,128)(2,1)S(1)} %bitcast.7), channel_id=1, source_target_pairs={{0,96},{32,0},{64,32},{96,64},{1,97},{33,1},{65,33},{97,65},{2,98}... | collective-permute-start | bytes 1572872 | tf_op jit(solution)/shard_map/project/ppermute | solution.py:444
  105.3 23.5 %collective-permute-start.4 = (bf16[8,128,256]{2,1,0:T(8,128)(2,1)S(1)}, bf16[8,128,256]{2,1,0:T(8,128)(2,1)S(1)}, u32[]{:S(2)}, u32[]{:S(2)}) collective-permute-start(bf16[8,128,256]{2,1,0:T(8,128)(2,1)S(1)} %bitcast.8), channel_id=1, source_target_pairs={{0,128},{128,0},{1,129},{129,1},{2,130},{130,2},{3,131},{131,3},{4... | collective-permute-start | bytes 1572872 | tf_op jit(solution)/shard_map/gram/ppermute | solution.py:437
  116.5 44.7 %copy-start.16 = (bf16[8,128,256]{2,1,0:T(8,128)(2,1)}, bf16[8,128,256]{2,1,0:T(8,128)(2,1)S(1)}, u32[]{:S(2)}) copy-start(bf16[8,128,256]{2,1,0:T(8,128)(2,1)S(1)} %collective-permute-done.1.refs_1_) | copy-start | bytes 1572868
  116.5 12.3 %collective-permute-start.2 = (bf16[8,128,256]{2,1,0:T(8,128)(2,1)S(1)}, bf16[8,128,256]{2,1,0:T(8,128)(2,1)}, u32[]{:S(2)}, u32[]{:S(2)}) collective-permute-start(bf16[8,128,256]{2,1,0:T(8,128)(2,1)S(1)} %collective-permute-done.1.refs_1_), channel_id=1, source_target_pairs={{0,96},{32,0},{64,32},{96,64},{1,97},{33,1},{65,33},{97,65},{2,98}... | collective-permute-start | bytes 1572872 | tf_op jit(solution)/shard_map/project/ppermute | solution.py:445
  142.4 43.3 %all-to-all-start.4 = ((bf16[16,128,384]{2,1,0:T(8,128)(2,1)}), bf16[16,128,384]{2,1,0:T(8,128)(2,1)S(1)}, u32[]{:S(2)}, u32[]{:S(2)}) async-start(bf16[16,128,384]{2,1,0:T(8,128)(2,1)} %broadcast_in_dim.5), calls=%async_computation.4 | async-start | bytes 3145728 | tf_op jit(solution)/shard_map/project/all_to_all | solution.py:416
  147.5 13.7 %collective-permute-start.3 = (bf16[8,128,256]{2,1,0:T(8,128)(2,1)S(1)}, bf16[8,128,256]{2,1,0:T(8,128)(2,1)S(1)}, u32[]{:S(2)}, u32[]{:S(2)}) collective-permute-start(bf16[8,128,256]{2,1,0:T(8,128)(2,1)S(1)} %bitcast.9), channel_id=1, source_target_pairs={{0,32},{32,64},{64,96},{96,0},{1,33},{33,65},{65,97},{97,1},{2,34}... | collective-permute-start | bytes 1572872 | tf_op jit(solution)/shard_map/project/ppermute | solution.py:443
  148.2 14.1 %collective-permute-start.5 = (bf16[8,128,256]{2,1,0:T(8,128)(2,1)S(1)}, bf16[8,128,256]{2,1,0:T(8,128)(2,1)S(1)}, u32[]{:S(2)}, u32[]{:S(2)}) collective-permute-start(bf16[8,128,256]{2,1,0:T(8,128)(2,1)S(1)} %copy-done.18), channel_id=1, source_target_pairs={{0,96},{32,0},{64,32},{96,64},{1,97},{33,1},{65,33},{97,65},{2,98}... | collective-permute-start | bytes 1572872 | tf_op jit(solution)/shard_map/project/ppermute | solution.py:444
  149.6 15.2 %collective-permute-start.8 = (bf16[8,128,256]{2,1,0:T(8,128)(2,1)S(1)}, bf16[8,128,256]{2,1,0:T(8,128)(2,1)S(1)}, u32[]{:S(2)}, u32[]{:S(2)}) collective-permute-start(bf16[8,128,256]{2,1,0:T(8,128)(2,1)S(1)} %bitcast.10), channel_id=1, source_target_pairs={{0,16},{16,0},{1,17},{17,1},{2,18},{18,2},{3,19},{19,3},{4,20},{20... | collective-permute-start | bytes 1572872 | tf_op jit(solution)/shard_map/project/ppermute | solution.py:450
  161.2 17.6 %copy-start.19 = (bf16[8,128,256]{2,1,0:T(8,128)(2,1)}, bf16[8,128,256]{2,1,0:T(8,128)(2,1)S(1)}, u32[]{:S(2)}) copy-start(bf16[8,128,256]{2,1,0:T(8,128)(2,1)S(1)} %collective-permute-done.3.refs_3_) | copy-start | bytes 1572868
  161.2 3.6 %collective-permute-start.11 = (bf16[8,128,256]{2,1,0:T(8,128)(2,1)S(1)}, bf16[8,128,256]{2,1,0:T(8,128)(2,1)S(1)}, u32[]{:S(2)}, u32[]{:S(2)}) collective-permute-start(bf16[8,128,256]{2,1,0:T(8,128)(2,1)S(1)} %collective-permute-done.3.refs_3_), channel_id=1, source_target_pairs={{0,16},{16,0},{1,17},{17,1},{2,18},{18,2},{3,19},{19,3},{4,20},{20... | collective-permute-start | bytes 1572872 | tf_op jit(solution)/shard_map/project/ppermute | solution.py:450
  161.2 4.1 %collective-permute-start.9 = (bf16[8,128,256]{2,1,0:T(8,128)(2,1)S(1)}, bf16[8,128,256]{2,1,0:T(8,128)(2,1)S(1)}, u32[]{:S(2)}, u32[]{:S(2)}) collective-permute-start(bf16[8,128,256]{2,1,0:T(8,128)(2,1)S(1)} %collective-permute-done.1.refs_1_), channel_id=1, source_target_pairs={{0,16},{16,0},{1,17},{17,1},{2,18},{18,2},{3,19},{19,3},{4,20},{20... | collective-permute-start | bytes 1572872 | tf_op jit(solution)/shard_map/project/ppermute | solution.py:450
  161.7 15.1 %collective-permute-start.7 = (bf16[8,128,256]{2,1,0:T(8,128)(2,1)S(1)}, bf16[8,128,256]{2,1,0:T(8,128)(2,1)S(1)}, u32[]{:S(2)}, u32[]{:S(2)}) collective-permute-start(bf16[8,128,256]{2,1,0:T(8,128)(2,1)S(1)} %copy-done.18), channel_id=1, source_target_pairs={{0,32},{32,64},{64,96},{96,0},{1,33},{33,65},{65,97},{97,1},{2,34}... | collective-permute-start | bytes 1572872 | tf_op jit(solution)/shard_map/project/ppermute | solution.py:443
  162.3 16.5 %copy-start.20 = (bf16[8,128,256]{2,1,0:T(8,128)(2,1)}, bf16[8,128,256]{2,1,0:T(8,128)(2,1)S(1)}, u32[]{:S(2)}) copy-start(bf16[8,128,256]{2,1,0:T(8,128)(2,1)S(1)} %collective-permute-done.5.refs_5_) | copy-start | bytes 1572868
  162.3 14.6 %collective-permute-start.6 = (bf16[8,128,256]{2,1,0:T(8,128)(2,1)S(1)}, bf16[8,128,256]{2,1,0:T(8,128)(2,1)S(1)}, u32[]{:S(2)}, u32[]{:S(2)}) collective-permute-start(bf16[8,128,256]{2,1,0:T(8,128)(2,1)S(1)} %collective-permute-done.5.refs_5_), channel_id=1, source_target_pairs={{0,96},{32,0},{64,32},{96,64},{1,97},{33,1},{65,33},{97,65},{2,98}... | collective-permute-start | bytes 1572872 | tf_op jit(solution)/shard_map/project/ppermute | solution.py:445
  164.8 12.6 %collective-permute-start.12 = (bf16[8,128,256]{2,1,0:T(8,128)(2,1)S(1)}, bf16[8,128,256]{2,1,0:T(8,128)(2,1)S(1)}, u32[]{:S(2)}, u32[]{:S(2)}) collective-permute-start(bf16[8,128,256]{2,1,0:T(8,128)(2,1)S(1)} %copy-done.18), channel_id=1, source_target_pairs={{0,16},{16,0},{1,17},{17,1},{2,18},{18,2},{3,19},{19,3},{4,20},{20... | collective-permute-start | bytes 1572872 | tf_op jit(solution)/shard_map/project/ppermute | solution.py:450
  164.8 12.6 %collective-permute-start.10 = (bf16[8,128,256]{2,1,0:T(8,128)(2,1)}, bf16[8,128,256]{2,1,0:T(8,128)(2,1)S(1)}, u32[]{:S(2)}, u32[]{:S(2)}) collective-permute-start(bf16[8,128,256]{2,1,0:T(8,128)(2,1)} %collective-permute-done.2.refs_2_), channel_id=1, source_target_pairs={{0,16},{16,0},{1,17},{17,1},{2,18},{18,2},{3,19},{19,3},{4,20},{20... | collective-permute-start | bytes 1572872 | tf_op jit(solution)/shard_map/project/ppermute | solution.py:450
  165.3 13.5 %collective-permute-start.13 = (bf16[8,128,256]{2,1,0:T(8,128)(2,1)S(1)}, bf16[8,128,256]{2,1,0:T(8,128)(2,1)S(1)}, u32[]{:S(2)}, u32[]{:S(2)}) collective-permute-start(bf16[8,128,256]{2,1,0:T(8,128)(2,1)S(1)} %collective-permute-done.5.refs_5_), channel_id=1, source_target_pairs={{0,16},{16,0},{1,17},{17,1},{2,18},{18,2},{3,19},{19,3},{4,20},{20... | collective-permute-start | bytes 1572872 | tf_op jit(solution)/shard_map/project/ppermute | solution.py:450
  176.9 1.9 collective-permute-start.15
  176.9 2.8 %collective-permute-start.14 = (bf16[8,128,256]{2,1,0:T(8,128)(2,1)S(1)}, bf16[8,128,256]{2,1,0:T(8,128)(2,1)}, u32[]{:S(2)}, u32[]{:S(2)}) collective-permute-start(bf16[8,128,256]{2,1,0:T(8,128)(2,1)S(1)} %collective-permute-done.6.refs_6_), channel_id=1, source_target_pairs={{0,16},{16,0},{1,17},{17,1},{2,18},{18,2},{3,19},{19,3},{4,20},{20... | collective-permute-start | bytes 1572872 | tf_op jit(solution)/shard_map/project/ppermute | solution.py:450
  212.4 4.5 %collective-permute-start.16 = (bf16[8,256,512]{2,1,0:T(8,128)(2,1)}, bf16[8,256,512]{2,1,0:T(8,128)(2,1)S(1)}, u32[]{:S(2)}, u32[]{:S(2)}) collective-permute-start(bf16[8,256,512]{2,1,0:T(8,128)(2,1)} %get-tuple-element.21), channel_id=1, source_target_pairs={{0,16},{16,0},{1,17},{17,1},{2,18},{18,2},{3,19},{19,3},{4,20},{20... | collective-permute-start | bytes 6291464 | tf_op jit(solution)/shard_map/sum/ppermute | solution.py:458
  219.1 31.8 %copy-start.3 = (f32[1,512,128]{2,1,0:T(8,128)S(1)}, f32[1,512,128]{2,1,0:T(8,128)}, u32[]{:S(2)}) copy-start(f32[1,512,128]{2,1,0:T(8,128)} %refs_0_.1) | copy-start | bytes 786436
  219.1 31.8 %copy-start.5 = (f32[1,128,512]{2,1,0:T(8,128)S(1)}, f32[1,128,512]{2,1,0:T(8,128)}, u32[]{:S(2)}) copy-start(f32[1,128,512]{2,1,0:T(8,128)} %refs_3_.1) | copy-start | bytes 786436
  219.2 31.8 %copy-start.6 = (f32[1,512,128]{2,1,0:T(8,128)S(1)}, f32[1,512,128]{2,1,0:T(8,128)}, u32[]{:S(2)}) copy-start(f32[1,512,128]{2,1,0:T(8,128)} %refs_1_.1) | copy-start | bytes 786436
  219.2 31.8 %copy-start.7 = (f32[1,512,128]{2,1,0:T(8,128)S(1)}, f32[1,512,128]{2,1,0:T(8,128)}, u32[]{:S(2)}) copy-start(f32[1,512,128]{2,1,0:T(8,128)} %refs_2_.1) | copy-start | bytes 786436
  219.2 31.7 %copy-start.8 = (f32[1,128,512]{2,1,0:T(8,128)S(1)}, f32[1,128,512]{2,1,0:T(8,128)}, u32[]{:S(2)}) copy-start(f32[1,128,512]{2,1,0:T(8,128)} %refs_4_.1) | copy-start | bytes 786436
  219.2 31.7 %copy-start.9 = (f32[1,128,512]{2,1,0:T(8,128)S(1)}, f32[1,128,512]{2,1,0:T(8,128)}, u32[]{:S(2)}) copy-start(f32[1,128,512]{2,1,0:T(8,128)} %refs_5_.1) | copy-start | bytes 786436
  (18 other events, 75.1 us)

commit v4 on v3

--- a/solution.py
+++ b/solution.py
@@ -249,6 +249,12 @@
     def arrived(layer):
         view = gram.at[pl.ds(0, (2 * layer + 1) * (RANK // 2)), pl.ds(0, 2 * RANK)]
         pltpu.make_async_copy(view, view, gram_sems.at[layer]).wait()
+
+    def leaving(half):
+        return (
+            pltpu.make_async_copy(shares.at[0, half], keep_ref.at[half], out_sems.at[0, half]),
+            pltpu.make_async_copy(shares.at[1, half], pass_ref.at[half], out_sems.at[1, half]),
+        )
 
     square = square_ref[...][:, :1]
     wide = rows_ref[...].astype(F32)
@@ -324,14 +330,12 @@
                 + nn(unit, weights[layer % 2, layer // 2, :RANK, :])
                 - share * layer_rows.astype(F32)
             )
-    last = [
-        pltpu.make_async_copy(shares.at[0], keep_ref, out_sems.at[0]),
-        pltpu.make_async_copy(shares.at[1], pass_ref, out_sems.at[1]),
-    ]
-    for copy in last:
-        copy.start()
-    for copy in last:
-        copy.wait()
+        if layer % 2 == 0:
+            for copy in leaving(layer // 2):
+                copy.start()
+    for half in range(HALF):
+        for copy in leaving(half):
+            copy.wait()
 
 
 def chain(index, gram, proj, square, near, far, rows, grads):
@@ -353,7 +357,7 @@
             pltpu.VMEM((LAYERS, CHUNK, RANK), F32),
             pltpu.SemaphoreType.DMA((LAYERS,)),
             pltpu.SemaphoreType.DMA((2,)),
-            pltpu.SemaphoreType.DMA((2,)),
+            pltpu.SemaphoreType.DMA((2, HALF)),
         ],
         compiler_params=params(56),
         cost_estimate=cost(4 * 2**30, 20 * 2**20),

time: 254 us -> 253 us (level)
  no operation moved by 1% of the time
where the time goes in v4:
time: 253 us; the launch traced here: 252 us
  blocking collectives  98.6 us (39%)
  waiting for transfers between devices  77.8 us (31%)
  Pallas kernels  33.5 us (13%)
  starting transfers between devices  25.9 us (10%)
  local copies, waits for them, and re-layouts  11.4 us (5%)
  other arithmetic  3.38 us (1%)
    all_to_all x3, blocking collectives, exchange(): return lax.all_to_all(value, axes, split_axis=0, concat_axis=0, tiled=True)  98.6 us
    all_to_all x3, waiting for transfers between devices, exchange(): return lax.all_to_all(value, axes, split_axis=0, concat_axis=0, tiled=True)  25.5 us
    pallas_call x1, Pallas kernels, chain(): pl.pallas_call(chain_kernel, out_shape=(side, side), in_specs=[SMEM] + [A...  24.4 us
    ppermute x2, waiting for transfers between devices, ring(): below = lax.ppermute(value, 'y', up)  22.9 us
    all_to_all x3, starting transfers between devices, exchange(): return lax.all_to_all(value, axes, split_axis=0, concat_axis=0, tiled=True)  14.3 us
    ppermute x1, waiting for transfers between devices, per_device(): other = lax.ppermute(blocks, 'xh', swap)  10.5 us
    ppermute x2, waiting for transfers between devices, ring(): above = lax.ppermute(value, 'y', down)  10.2 us
    unnamed x60, local copies, waits for them, and re-layouts  7.8 us
  transfers between devices with their start and end apart: 20, of which 11 were waited for; matrix products, arithmetic and copies ran while one was open for 1% of the time, Pallas kernels for 2%

profile of v4, /device:TPU:8, one launch (start us, length us, event | category | flops | bytes accessed | tf_op | source)
XLA Modules:
  0.0 251.6 jit_solution(7233769693667194071)
XLA Ops:
  1.3 0.9 copy-done.2
  2.3 0.9 copy-done.4
  3.4 33.7 %all_to_all.30.near_ref.refs_18_ = bf16[8,256,512]{2,1,0:T(8,128)(2,1)S(1)} all-to-all(bf16[8,256,512]{2,1,0:T(8,128)(2,1)S(1)} %weights.1), channel_id=1, replica_groups=mesh['xh'=2,'y'=4,'c'=2,'xl'=2,'z'=8] {'xh','y'}, dimensions={0} | all-to-all | bytes 4194304 | tf_op jit(solution)/shard_map/weights/all_to_all | solution.py:420
  37.2 1.3 constant_dynamic-slice_fusion
  38.6 2.9 %collective-permute-done.far_ref.refs_19_ = bf16[8,256,512]{2,1,0:T(8,128)(2,1)} collective-permute-done((bf16[8,256,512]{2,1,0:T(8,128)(2,1)S(1)}, bf16[8,256,512]{2,1,0:T(8,128)(2,1)}, u32[]{:S(2)}, u32[]{:S(2)}) %collective-permute-start) | collective-permute-done | bytes 2097184 | tf_op jit(solution)/shard_map/weights/ppermute | solution.py:427
  41.4 3.1 %gram.1 = bf16[16,112,256]{2,1,0:T(8,128)(2,1)S(1)} custom-call(s32[4]{0:T(128)S(1)} %pad_add_fusion.index_ref, bf16[8,256,512]{2,1,0:T(8,128)(2,1)S(1)} %all_to_all.30.near_ref.refs_18_, bf16[8,256,512]{2,1,0:T(8,128)(2,1)} %collective-permute-done.far_ref.refs_19_, bf16[16,8192]{1,0:T(8,128)(2,1)S(1)} %pad_maximum_fusion.both_ref), custom_call_target="tpu_custom_call" | custom-call | flops 268435456 | bytes 6291456 | tf_op jit(solution)/shard_map/gram/pallas_call | solution.py:136
  44.5 33.1 %all_to_all.31.packed_ref = bf16[16,112,256]{2,1,0:T(8,128)(2,1)S(1)} all-to-all(bf16[16,112,256]{2,1,0:T(8,128)(2,1)S(1)} %gram.1), channel_id=1, replica_groups=mesh['xh'=2,'y'=4,'c'=2,'xl'=2,'z'=8] {'xl','z'}, dimensions={0} | all-to-all | bytes 1835008 | tf_op jit(solution)/shard_map/gram/all_to_all | solution.py:420
  78.6 4.5 %all-to-all-start.2 = ((bf16[16,64,256]{2,1,0:T(8,128)(2,1)}), bf16[16,64,256]{2,1,0:T(8,128)(2,1)S(1)}, u32[]{:S(2)}, u32[]{:S(2)}) async-start(bf16[16,64,256]{2,1,0:T(8,128)(2,1)} %broadcast_in_dim.4), calls=%async_computation.2 | async-start | bytes 1048576 | tf_op jit(solution)/shard_map/gram/all_to_all | solution.py:420
  83.1 4.2 %project.1 = (bf16[16,128,384]{2,1,0:T(8,128)(2,1)S(1)}, bf16[128,512]{1,0:T(8,128)(2,1)S(1)}, bf16[128,512]{1,0:T(8,128)(2,1)S(1)}, f32[128,128]{1,0:T(8,128)S(1)}) custom-call(s32[4]{0:T(128)S(1)} %pad_add_fusion.index_ref, bf16[16,112,256]{2,1,0:T(8,128)(2,1)S(1)} %all_to_all.31.packed_ref, bf16[8,256,512]{2,1,0:T(8,128)(2,1)S(1)} %all_to_all.30.near_ref.refs_18_, ...), custom_call_target="tpu_custom_call" | custom-call | flops 805306368 | bytes 7340032 | tf_op jit(solution)/shard_map/project/pallas_call | solution.py:174
  87.4 1.2 copy-done.1
  90.5 8.2 %all-to-all-done.2 = bf16[16,64,256]{2,1,0:T(8,128)(2,1)S(1)} async-done(((bf16[16,64,256]{2,1,0:T(8,128)(2,1)}), bf16[16,64,256]{2,1,0:T(8,128)(2,1)S(1)}, u32[]{:S(2)}, u32[]{:S(2)}) %all-to-all-start.2) | async-done | bytes 524320 | tf_op jit(solution)/shard_map/gram/all_to_all | solution.py:420
  98.8 4.7 %all-to-all-start.3 = ((bf16[16,128,384]{2,1,0:T(8,128)(2,1)}), bf16[16,128,384]{2,1,0:T(8,128)(2,1)S(1)}, u32[]{:S(2)}, u32[]{:S(2)}) async-start(bf16[16,128,384]{2,1,0:T(8,128)(2,1)} %copy-done.1), calls=%async_computation.3 | async-start | bytes 3145728 | tf_op jit(solution)/shard_map/project/all_to_all | solution.py:420
  103.4 1.9 collective-permute-start.1
  105.3 1.0 collective-permute-start.4
  106.3 10.2 %collective-permute-done.1.refs_1_ = bf16[8,128,256]{2,1,0:T(8,128)(2,1)S(1)} collective-permute-done((bf16[8,128,256]{2,1,0:T(8,128)(2,1)S(1)}, bf16[8,128,256]{2,1,0:T(8,128)(2,1)S(1)}, u32[]{:S(2)}, u32[]{:S(2)}) %collective-permute-start.1) | collective-permute-done | bytes 524320 | tf_op jit(solution)/shard_map/project/ppermute | solution.py:448
  116.5 1.8 collective-permute-start.2
  118.3 10.5 %collective-permute-done.4.refs_4_ = bf16[8,128,256]{2,1,0:T(8,128)(2,1)S(1)} collective-permute-done((bf16[8,128,256]{2,1,0:T(8,128)(2,1)S(1)}, bf16[8,128,256]{2,1,0:T(8,128)(2,1)S(1)}, u32[]{:S(2)}, u32[]{:S(2)}) %collective-permute-start.4) | collective-permute-done | bytes 524320 | tf_op jit(solution)/shard_map/gram/ppermute | solution.py:441
  129.6 11.2 %all-to-all-done.3 = bf16[16,128,384]{2,1,0:T(8,128)(2,1)S(1)} async-done(((bf16[16,128,384]{2,1,0:T(8,128)(2,1)}), bf16[16,128,384]{2,1,0:T(8,128)(2,1)S(1)}, u32[]{:S(2)}, u32[]{:S(2)}) %all-to-all-start.3) | async-done | bytes 1572896 | tf_op jit(solution)/shard_map/project/all_to_all | solution.py:420
  141.0 1.4 broadcast_in_dim.5
  142.4 5.1 %all-to-all-start.4 = ((bf16[16,128,384]{2,1,0:T(8,128)(2,1)}), bf16[16,128,384]{2,1,0:T(8,128)(2,1)S(1)}, u32[]{:S(2)}, u32[]{:S(2)}) async-start(bf16[16,128,384]{2,1,0:T(8,128)(2,1)} %broadcast_in_dim.5), calls=%async_computation.4 | async-start | bytes 3145728 | tf_op jit(solution)/shard_map/project/all_to_all | solution.py:420
  148.2 1.4 collective-permute-start.5
  149.6 11.6 %collective-permute-done.3.refs_3_ = bf16[8,128,256]{2,1,0:T(8,128)(2,1)S(1)} collective-permute-done((bf16[8,128,256]{2,1,0:T(8,128)(2,1)S(1)}, bf16[8,128,256]{2,1,0:T(8,128)(2,1)S(1)}, u32[]{:S(2)}, u32[]{:S(2)}) %collective-permute-start.3) | collective-permute-done | bytes 524320 | tf_op jit(solution)/shard_map/project/ppermute | solution.py:447
  162.3 2.5 collective-permute-start.6
  165.6 11.3 %collective-permute-done.7.refs_7_ = bf16[8,128,256]{2,1,0:T(8,128)(2,1)S(1)} collective-permute-done((bf16[8,128,256]{2,1,0:T(8,128)(2,1)S(1)}, bf16[8,128,256]{2,1,0:T(8,128)(2,1)S(1)}, u32[]{:S(2)}, u32[]{:S(2)}) %collective-permute-start.7) | collective-permute-done | bytes 524320 | tf_op jit(solution)/shard_map/project/ppermute | solution.py:447
  177.4 1.4 collective-permute-done.15.refs_15_
  179.7 6.1 %all-to-all-done.4.refs_16_ = bf16[16,128,384]{2,1,0:T(8,128)(2,1)S(1)} async-done(((bf16[16,128,384]{2,1,0:T(8,128)(2,1)}), bf16[16,128,384]{2,1,0:T(8,128)(2,1)S(1)}, u32[]{:S(2)}, u32[]{:S(2)}) %all-to-all-start.4) | async-done | bytes 1572896 | tf_op jit(solution)/shard_map/project/all_to_all | solution.py:420
  185.8 1.1 copy-done.14
  186.9 24.4 %chain.1 = (bf16[8,256,512]{2,1,0:T(8,128)(2,1)}, bf16[8,256,512]{2,1,0:T(8,128)(2,1)}) custom-call(s32[4]{0:T(128)} %copy-done.10, bf16[8,128,256]{2,1,0:T(8,128)(2,1)} %bitcast.11, bf16[8,128,256]{2,1,0:T(8,128)(2,1)} %copy-done.16, bf16[8,128,256]{2,1,0:T(8,128)(2,1)} %collective-permute-done.2.refs_2_, bf16[8,128,256]{2,1,0:T(8,128)(2,1)} %copy-done.19, ...), custom_call_target="tpu_custom_call" | custom-call | flops 4294967296 | bytes 20971520 | tf_op jit(solution)/shard_map/chain/pallas_call | solution.py:343
  211.4 4.4 %collective-permute-done.16 = bf16[8,256,512]{2,1,0:T(8,128)(2,1)S(1)} collective-permute-done((bf16[8,256,512]{2,1,0:T(8,128)(2,1)}, bf16[8,256,512]{2,1,0:T(8,128)(2,1)S(1)}, u32[]{:S(2)}, u32[]{:S(2)}) %collective-permute-start.16) | collective-permute-done | bytes 2097184 | tf_op jit(solution)/shard_map/sum/ppermute | solution.py:462
  215.8 2.3 add_convert_fusion
  218.2 31.7 %all_to_all.32.parts_ref = bf16[8,256,512]{2,1,0:T(8,128)(2,1)S(1)} all-to-all(bf16[8,256,512]{2,1,0:T(8,128)(2,1)S(1)} %add_convert_fusion), channel_id=1, replica_groups=mesh['xh'=2,'y'=4,'c'=2,'xl'=2,'z'=8] {'xh','y'}, dimensions={0} | all-to-all | bytes 4194304 | tf_op jit(solution)/shard_map/sum/all_to_all | solution.py:420
  249.9 1.6 adam.1
  (85 shorter events, 8.9 us)
Async XLA Ops:
  37.1 46.0 %copy-start = (bf16[8,256,512]{2,1,0:T(8,128)(2,1)}, bf16[8,256,512]{2,1,0:T(8,128)(2,1)S(1)}, u32[]{:S(2)}) copy-start(bf16[8,256,512]{2,1,0:T(8,128)(2,1)S(1)} %all_to_all.30.near_ref.refs_18_) | copy-start | bytes 6291460
  37.1 4.3 %collective-permute-start = (bf16[8,256,512]{2,1,0:T(8,128)(2,1)S(1)}, bf16[8,256,512]{2,1,0:T(8,128)(2,1)}, u32[]{:S(2)}, u32[]{:S(2)}) collective-permute-start(bf16[8,256,512]{2,1,0:T(8,128)(2,1)S(1)} %all_to_all.30.near_ref.refs_18_), channel_id=1, source_target_pairs={{0,16},{16,0},{1,17},{17,1},{2,18},{18,2},{3,19},{19,3},{4,20},{20... | collective-permute-start | bytes 6291464 | tf_op jit(solution)/shard_map/weights/ppermute | solution.py:427
  37.2 45.9 %copy-start.10 = (s32[4]{0:T(128)}, s32[4]{0:T(128)S(1)}, u32[]{:S(2)}) copy-start(s32[4]{0:T(128)S(1)} %pad_add_fusion.index_ref) | copy-start | bytes 52
  78.6 20.2 %all-to-all-start.2 = ((bf16[16,64,256]{2,1,0:T(8,128)(2,1)}), bf16[16,64,256]{2,1,0:T(8,128)(2,1)S(1)}, u32[]{:S(2)}, u32[]{:S(2)}) async-start(bf16[16,64,256]{2,1,0:T(8,128)(2,1)} %broadcast_in_dim.4), calls=%async_computation.2 | async-start | bytes 1048576 | tf_op jit(solution)/shard_map/gram/all_to_all | solution.py:420
  98.8 50.9 %copy-start.15 = (bf16[16,64,256]{2,1,0:T(8,128)(2,1)}, bf16[16,64,256]{2,1,0:T(8,128)(2,1)S(1)}, u32[]{:S(2)}) copy-start(bf16[16,64,256]{2,1,0:T(8,128)(2,1)S(1)} %all-to-all-done.2) | copy-start | bytes 1572868
  98.8 42.0 %all-to-all-start.3 = ((bf16[16,128,384]{2,1,0:T(8,128)(2,1)}), bf16[16,128,384]{2,1,0:T(8,128)(2,1)S(1)}, u32[]{:S(2)}, u32[]{:S(2)}) async-start(bf16[16,128,384]{2,1,0:T(8,128)(2,1)} %copy-done.1), calls=%async_computation.3 | async-start | bytes 3145728 | tf_op jit(solution)/shard_map/project/all_to_all | solution.py:420
  103.4 13.0 %collective-permute-start.1 = (bf16[8,128,256]{2,1,0:T(8,128)(2,1)S(1)}, bf16[8,128,256]{2,1,0:T(8,128)(2,1)S(1)}, u32[]{:S(2)}, u32[]{:S(2)}) collective-permute-start(bf16[8,128,256]{2,1,0:T(8,128)(2,1)S(1)} %bitcast.7), channel_id=1, source_target_pairs={{0,96},{32,0},{64,32},{96,64},{1,97},{33,1},{65,33},{97,65},{2,98}... | collective-permute-start | bytes 1572872 | tf_op jit(solution)/shard_map/project/ppermute | solution.py:448
  105.3 23.5 %collective-permute-start.4 = (bf16[8,128,256]{2,1,0:T(8,128)(2,1)S(1)}, bf16[8,128,256]{2,1,0:T(8,128)(2,1)S(1)}, u32[]{:S(2)}, u32[]{:S(2)}) collective-permute-start(bf16[8,128,256]{2,1,0:T(8,128)(2,1)S(1)} %bitcast.8), channel_id=1, source_target_pairs={{0,128},{128,0},{1,129},{129,1},{2,130},{130,2},{3,131},{131,3},{4... | collective-permute-start | bytes 1572872 | tf_op jit(solution)/shard_map/gram/ppermute | solution.py:441
  116.5 44.7 %copy-start.16 = (bf16[8,128,256]{2,1,0:T(8,128)(2,1)}, bf16[8,128,256]{2,1,0:T(8,128)(2,1)S(1)}, u32[]{:S(2)}) copy-start(bf16[8,128,256]{2,1,0:T(8,128)(2,1)S(1)} %collective-permute-done.1.refs_1_) | copy-start | bytes 1572868
  116.5 12.3 %collective-permute-start.2 = (bf16[8,128,256]{2,1,0:T(8,128)(2,1)S(1)}, bf16[8,128,256]{2,1,0:T(8,128)(2,1)}, u32[]{:S(2)}, u32[]{:S(2)}) collective-permute-start(bf16[8,128,256]{2,1,0:T(8,128)(2,1)S(1)} %collective-permute-done.1.refs_1_), channel_id=1, source_target_pairs={{0,96},{32,0},{64,32},{96,64},{1,97},{33,1},{65,33},{97,65},{2,98}... | collective-permute-start | bytes 1572872 | tf_op jit(solution)/shard_map/project/ppermute | solution.py:449
  142.4 43.3 %all-to-all-start.4 = ((bf16[16,128,384]{2,1,0:T(8,128)(2,1)}), bf16[16,128,384]{2,1,0:T(8,128)(2,1)S(1)}, u32[]{:S(2)}, u32[]{:S(2)}) async-start(bf16[16,128,384]{2,1,0:T(8,128)(2,1)} %broadcast_in_dim.5), calls=%async_computation.4 | async-start | bytes 3145728 | tf_op jit(solution)/shard_map/project/all_to_all | solution.py:420
  147.5 13.7 %collective-permute-start.3 = (bf16[8,128,256]{2,1,0:T(8,128)(2,1)S(1)}, bf16[8,128,256]{2,1,0:T(8,128)(2,1)S(1)}, u32[]{:S(2)}, u32[]{:S(2)}) collective-permute-start(bf16[8,128,256]{2,1,0:T(8,128)(2,1)S(1)} %bitcast.9), channel_id=1, source_target_pairs={{0,32},{32,64},{64,96},{96,0},{1,33},{33,65},{65,97},{97,1},{2,34}... | collective-permute-start | bytes 1572872 | tf_op jit(solution)/shard_map/project/ppermute | solution.py:447
  148.2 14.1 %collective-permute-start.5 = (bf16[8,128,256]{2,1,0:T(8,128)(2,1)S(1)}, bf16[8,128,256]{2,1,0:T(8,128)(2,1)S(1)}, u32[]{:S(2)}, u32[]{:S(2)}) collective-permute-start(bf16[8,128,256]{2,1,0:T(8,128)(2,1)S(1)} %copy-done.18), channel_id=1, source_target_pairs={{0,96},{32,0},{64,32},{96,64},{1,97},{33,1},{65,33},{97,65},{2,98}... | collective-permute-start | bytes 1572872 | tf_op jit(solution)/shard_map/project/ppermute | solution.py:448
  149.6 15.2 %collective-permute-start.8 = (bf16[8,128,256]{2,1,0:T(8,128)(2,1)S(1)}, bf16[8,128,256]{2,1,0:T(8,128)(2,1)S(1)}, u32[]{:S(2)}, u32[]{:S(2)}) collective-permute-start(bf16[8,128,256]{2,1,0:T(8,128)(2,1)S(1)} %bitcast.10), channel_id=1, source_target_pairs={{0,16},{16,0},{1,17},{17,1},{2,18},{18,2},{3,19},{19,3},{4,20},{20... | collective-permute-start | bytes 1572872 | tf_op jit(solution)/shard_map/project/ppermute | solution.py:454
  161.2 17.6 %copy-start.19 = (bf16[8,128,256]{2,1,0:T(8,128)(2,1)}, bf16[8,128,256]{2,1,0:T(8,128)(2,1)S(1)}, u32[]{:S(2)}) copy-start(bf16[8,128,256]{2,1,0:T(8,128)(2,1)S(1)} %collective-permute-done.3.refs_3_) | copy-start | bytes 1572868
  161.2 3.6 %collective-permute-start.11 = (bf16[8,128,256]{2,1,0:T(8,128)(2,1)S(1)}, bf16[8,128,256]{2,1,0:T(8,128)(2,1)S(1)}, u32[]{:S(2)}, u32[]{:S(2)}) collective-permute-start(bf16[8,128,256]{2,1,0:T(8,128)(2,1)S(1)} %collective-permute-done.3.refs_3_), channel_id=1, source_target_pairs={{0,16},{16,0},{1,17},{17,1},{2,18},{18,2},{3,19},{19,3},{4,20},{20... | collective-permute-start | bytes 1572872 | tf_op jit(solution)/shard_map/project/ppermute | solution.py:454
  161.2 4.1 %collective-permute-start.9 = (bf16[8,128,256]{2,1,0:T(8,128)(2,1)S(1)}, bf16[8,128,256]{2,1,0:T(8,128)(2,1)S(1)}, u32[]{:S(2)}, u32[]{:S(2)}) collective-permute-start(bf16[8,128,256]{2,1,0:T(8,128)(2,1)S(1)} %collective-permute-done.1.refs_1_), channel_id=1, source_target_pairs={{0,16},{16,0},{1,17},{17,1},{2,18},{18,2},{3,19},{19,3},{4,20},{20... | collective-permute-start | bytes 1572872 | tf_op jit(solution)/shard_map/project/ppermute | solution.py:454
  161.7 15.1 %collective-permute-start.7 = (bf16[8,128,256]{2,1,0:T(8,128)(2,1)S(1)}, bf16[8,128,256]{2,1,0:T(8,128)(2,1)S(1)}, u32[]{:S(2)}, u32[]{:S(2)}) collective-permute-start(bf16[8,128,256]{2,1,0:T(8,128)(2,1)S(1)} %copy-done.18), channel_id=1, source_target_pairs={{0,32},{32,64},{64,96},{96,0},{1,33},{33,65},{65,97},{97,1},{2,34}... | collective-permute-start | bytes 1572872 | tf_op jit(solution)/shard_map/project/ppermute | solution.py:447
  162.3 16.5 %copy-start.20 = (bf16[8,128,256]{2,1,0:T(8,128)(2,1)}, bf16[8,128,256]{2,1,0:T(8,128)(2,1)S(1)}, u32[]{:S(2)}) copy-start(bf16[8,128,256]{2,1,0:T(8,128)(2,1)S(1)} %collective-permute-done.5.refs_5_) | copy-start | bytes 1572868
  162.3 14.6 %collective-permute-start.6 = (bf16[8,128,256]{2,1,0:T(8,128)(2,1)S(1)}, bf16[8,128,256]{2,1,0:T(8,128)(2,1)S(1)}, u32[]{:S(2)}, u32[]{:S(2)}) collective-permute-start(bf16[8,128,256]{2,1,0:T(8,128)(2,1)S(1)} %collective-permute-done.5.refs_5_), channel_id=1, source_target_pairs={{0,96},{32,0},{64,32},{96,64},{1,97},{33,1},{65,33},{97,65},{2,98}... | collective-permute-start | bytes 1572872 | tf_op jit(solution)/shard_map/project/ppermute | solution.py:449
  164.8 12.6 %collective-permute-start.12 = (bf16[8,128,256]{2,1,0:T(8,128)(2,1)S(1)}, bf16[8,128,256]{2,1,0:T(8,128)(2,1)S(1)}, u32[]{:S(2)}, u32[]{:S(2)}) collective-permute-start(bf16[8,128,256]{2,1,0:T(8,128)(2,1)S(1)} %copy-done.18), channel_id=1, source_target_pairs={{0,16},{16,0},{1,17},{17,1},{2,18},{18,2},{3,19},{19,3},{4,20},{20... | collective-permute-start | bytes 1572872 | tf_op jit(solution)/shard_map/project/ppermute | solution.py:454
  164.8 12.6 %collective-permute-start.10 = (bf16[8,128,256]{2,1,0:T(8,128)(2,1)}, bf16[8,128,256]{2,1,0:T(8,128)(2,1)S(1)}, u32[]{:S(2)}, u32[]{:S(2)}) collective-permute-start(bf16[8,128,256]{2,1,0:T(8,128)(2,1)} %collective-permute-done.2.refs_2_), channel_id=1, source_target_pairs={{0,16},{16,0},{1,17},{17,1},{2,18},{18,2},{3,19},{19,3},{4,20},{20... | collective-permute-start | bytes 1572872 | tf_op jit(solution)/shard_map/project/ppermute | solution.py:454
  165.3 13.5 %collective-permute-start.13 = (bf16[8,128,256]{2,1,0:T(8,128)(2,1)S(1)}, bf16[8,128,256]{2,1,0:T(8,128)(2,1)S(1)}, u32[]{:S(2)}, u32[]{:S(2)}) collective-permute-start(bf16[8,128,256]{2,1,0:T(8,128)(2,1)S(1)} %collective-permute-done.5.refs_5_), channel_id=1, source_target_pairs={{0,16},{16,0},{1,17},{17,1},{2,18},{18,2},{3,19},{19,3},{4,20},{20... | collective-permute-start | bytes 1572872 | tf_op jit(solution)/shard_map/project/ppermute | solution.py:454
  176.9 1.9 collective-permute-start.15
  176.9 2.8 %collective-permute-start.14 = (bf16[8,128,256]{2,1,0:T(8,128)(2,1)S(1)}, bf16[8,128,256]{2,1,0:T(8,128)(2,1)}, u32[]{:S(2)}, u32[]{:S(2)}) collective-permute-start(bf16[8,128,256]{2,1,0:T(8,128)(2,1)S(1)} %collective-permute-done.6.refs_6_), channel_id=1, source_target_pairs={{0,16},{16,0},{1,17},{17,1},{2,18},{18,2},{3,19},{19,3},{4,20},{20... | collective-permute-start | bytes 1572872 | tf_op jit(solution)/shard_map/project/ppermute | solution.py:454
  211.3 4.5 %collective-permute-start.16 = (bf16[8,256,512]{2,1,0:T(8,128)(2,1)}, bf16[8,256,512]{2,1,0:T(8,128)(2,1)S(1)}, u32[]{:S(2)}, u32[]{:S(2)}) collective-permute-start(bf16[8,256,512]{2,1,0:T(8,128)(2,1)} %get-tuple-element.21), channel_id=1, source_target_pairs={{0,16},{16,0},{1,17},{17,1},{2,18},{18,2},{3,19},{19,3},{4,20},{20... | collective-permute-start | bytes 6291464 | tf_op jit(solution)/shard_map/sum/ppermute | solution.py:462
  218.1 31.8 %copy-start.3 = (f32[1,512,128]{2,1,0:T(8,128)S(1)}, f32[1,512,128]{2,1,0:T(8,128)}, u32[]{:S(2)}) copy-start(f32[1,512,128]{2,1,0:T(8,128)} %refs_0_.1) | copy-start | bytes 786436
  218.1 31.8 %copy-start.5 = (f32[1,128,512]{2,1,0:T(8,128)S(1)}, f32[1,128,512]{2,1,0:T(8,128)}, u32[]{:S(2)}) copy-start(f32[1,128,512]{2,1,0:T(8,128)} %refs_3_.1) | copy-start | bytes 786436
  218.1 31.8 %copy-start.6 = (f32[1,512,128]{2,1,0:T(8,128)S(1)}, f32[1,512,128]{2,1,0:T(8,128)}, u32[]{:S(2)}) copy-start(f32[1,512,128]{2,1,0:T(8,128)} %refs_1_.1) | copy-start | bytes 786436
  218.1 31.8 %copy-start.7 = (f32[1,512,128]{2,1,0:T(8,128)S(1)}, f32[1,512,128]{2,1,0:T(8,128)}, u32[]{:S(2)}) copy-start(f32[1,512,128]{2,1,0:T(8,128)} %refs_2_.1) | copy-start | bytes 786436
  218.1 31.7 %copy-start.8 = (f32[1,128,512]{2,1,0:T(8,128)S(1)}, f32[1,128,512]{2,1,0:T(8,128)}, u32[]{:S(2)}) copy-start(f32[1,128,512]{2,1,0:T(8,128)} %refs_4_.1) | copy-start | bytes 786436
  218.2 31.7 %copy-start.9 = (f32[1,128,512]{2,1,0:T(8,128)S(1)}, f32[1,128,512]{2,1,0:T(8,128)}, u32[]{:S(2)}) copy-start(f32[1,128,512]{2,1,0:T(8,128)} %refs_5_.1) | copy-start | bytes 786436
  (18 other events, 75.1 us)
